TPU v7x, 32 devices: a whole 2x2x4 slice. The times are simulated.
32 devices in a mesh: groups: 2 (over x), seg: 4 (over z), blk: 4 (over y, core).
Axes of the slice: x: 2, y: 2, z: 4, core: 2. Of those that a mesh axis runs over, the one named last changes fastest.
Arguments:
- base_state: float32 [16, 20, 32, 128], P(('groups', 'seg'), None, 'blk'), parts along dimension 0, may hold values from -6 to 6
- direction: float32 [16, 20, 32, 128], P(('groups', 'seg'), None, 'blk'), parts along dimension 0, may hold values from -6 to 6
- coupling: float32 [40, 20], P('groups'), parts along dimension 0, may hold values from -1.25 to 1.25
- tiles: bfloat16 [8, 32, 16, 128, 128], P('seg', 'blk'), may hold values from -0.15625 to 0.15625
- columns: int32 [8, 32, 16], P('seg', 'blk'), may hold values from 0 to 31, as said below
- wet: int32 [32, 128], P('blk'), may hold values 0 or 1
- basis: float32 [8, 16, 20, 32, 128], P(None, ('groups', 'seg'), None, 'blk'), parts along dimension 1, may hold values from -0.0078125 to 0.0078125
Outputs:
- orthogonal: float32 [16, 20, 32, 128], P(('groups', 'seg'), None, 'blk'), parts along dimension 0
- coefficients: float32 [18], P('groups'), parts along dimension 0
There are 2 independent parts, one for each index of `groups`. A program takes and returns all parts, laid end to end along the dimension named above; an argument that names none is the same for every part. Nothing has to cross between parts.
Inputs may be any that keep to these rules, and one draw needn't show every extreme that they name: columns[s, r, k] = (r + d) mod 32 for some whole d with -2 <= d <= 2; in every segment some entry has d = 2 and some has d = -2.
All inputs are finite; a program needn't handle non-finite values. No bound on the sum of `wet` on one device may be relied on, other than what follows from the above.
Results may differ from a plain program's by a relative error of at most 0.04.
Values may be sent and summed in bfloat16 or wider, within the bound.
A program may use at most 128 MiB of HBM per device.

v0:
```python
import functools

import jax
import jax.numpy as jnp
from jax import lax
from jax.experimental import pallas as pl
from jax.experimental.pallas import tpu as pltpu
from jax.sharding import PartitionSpec as P

STEPS = 18
MESH = pl.DeviceIdType.MESH
REACH = 2
PAD = 32


def merge_kernel(total, rows, stored, cols_ref, tiles_ref, w_ref, acc):
    s, g = pl.program_id(0), pl.program_id(1)
    first = lax.axis_index("blk") * rows
    acc[...] = jnp.zeros_like(acc)
    wide = 2 * REACH + 2
    for j in range(2):
        row = 2 * g + j

        def add(k, unused):
            col = cols_ref[(s * rows + row) * stored + k]
            d = lax.rem(col - first - row + (REACH + total), total)
            at = j * wide + j + d
            acc[at] += tiles_ref[0, j, k].astype(jnp.float32)
            return unused

        lax.fori_loop(0, stored, add, 0, unroll=2)
    size = acc.shape[1]
    for j in range(2):
        for c in range(wide):
            w_ref[0, 0, c * size:(c + 1) * size, j * size:(j + 1) * size] = (
                acc[j * wide + c].T.astype(jnp.bfloat16)
            )


def steps_kernel(
    dims, base_ref, dir_ref, coup_ref, wet_ref, w_hbm, basis_hbm, orth_ref, coef_ref,
    w, basis, drive, slope, cc, wetf, follow, native, part1, part2,
    send_sem, recv_sem, follow_sem, load_sem, red_sem1, red_sem2,
):
    segs, tracers, rows, points, kry, n_seg, n_blk, entries = dims
    pairs = rows // 2
    per = tracers * rows
    me_seg, me_blk = lax.axis_index("seg"), lax.axis_index("blk")
    left, right = lax.rem(me_blk + n_blk - 1, n_blk), lax.rem(me_blk + 1, n_blk)

    w_copy = pltpu.make_async_copy(w_hbm, w, load_sem.at[0])
    basis_copy = pltpu.make_async_copy(basis_hbm, basis, load_sem.at[1])
    w_copy.start()
    basis_copy.start()

    barrier = pltpu.get_barrier_semaphore()
    for i in range(1, n_blk):
        pl.semaphore_signal(barrier, inc=1, device_id={"blk": lax.rem(me_blk + i, n_blk)}, device_id_type=MESH)
    for i in range(1, n_seg):
        pl.semaphore_signal(barrier, inc=1, device_id={"seg": lax.rem(me_seg + i, n_seg)}, device_id_type=MESH)

    c = 0.5 * coup_ref[...]
    high = c.astype(jnp.bfloat16)
    low = (c - high.astype(jnp.float32)).astype(jnp.bfloat16)
    cc[...] = jnp.zeros_like(cc)
    cc[:tracers, 0:tracers] = high.astype(jnp.float32)
    cc[:tracers, PAD:PAD + tracers] = low.astype(jnp.float32)
    mix = cc[...].astype(jnp.bfloat16)
    slope[...] = jnp.zeros_like(slope)
    native[...] = jnp.zeros_like(native)
    for r in range(rows):
        lanes = slice(r * points, (r + 1) * points)
        wetf[:, lanes] = wet_ref[r:r + 1, :].astype(jnp.float32)
        for s in range(segs):
            t = jnp.tanh(base_ref[pl.ds(s * per + r, tracers, stride=rows), :])
            slope[s, :tracers, lanes] = 1.0 - t * t
            native[s, :tracers, lanes] = dir_ref[pl.ds(s * per + r, tracers, stride=rows), :]

    def lanes_of(g, blocks=2):
        return slice(2 * g * points, (2 * g + blocks) * points)

    def force(u, s, g, slot):
        x = slope[s, :, lanes_of(g)] * u
        xh = x.astype(jnp.bfloat16)
        stack = jnp.concatenate([xh, xh], axis=0)
        d = u + jnp.dot(mix, stack, preferred_element_type=jnp.float32)
        drive[slot, s, :, lanes_of(g + 1)] = d.astype(jnp.bfloat16)

    def move(s, g, slot):
        m = jnp.dot(
            drive[slot, s, :, lanes_of(g, 2 * REACH + 2)], w[s, g],
            preferred_element_type=jnp.float32,
        )
        return m * wetf[:, lanes_of(g)]

    def halos(s, slot):
        return [
            pltpu.make_async_remote_copy(
                src_ref=drive.at[slot, s, :, lanes_of(1)],
                dst_ref=drive.at[slot, s, :, lanes_of(pairs + 1)],
                send_sem=send_sem.at[slot, s, 0], recv_sem=recv_sem.at[slot, s, 0],
                device_id={"blk": left}, device_id_type=MESH,
            ),
            pltpu.make_async_remote_copy(
                src_ref=drive.at[slot, s, :, lanes_of(pairs)],
                dst_ref=drive.at[slot, s, :, lanes_of(0)],
                send_sem=send_sem.at[slot, s, 1], recv_sem=recv_sem.at[slot, s, 1],
                device_id={"blk": right}, device_id_type=MESH,
            ),
        ]

    edges, inner = (0, pairs - 1), range(1, pairs - 1)
    for s in range(segs):
        for g in edges:
            force(native[s, :, lanes_of(g)], s, g, 0)
    pl.semaphore_wait(barrier, n_blk + n_seg - 2)
    for s in range(segs):
        for h in halos(s, 0):
            h.start()
    follow_copy = pltpu.make_async_remote_copy(
        src_ref=dir_ref.at[0:per], dst_ref=follow, send_sem=follow_sem.at[0], recv_sem=follow_sem.at[1],
        device_id={"seg": lax.rem(me_seg + n_seg - 1, n_seg)}, device_id_type=MESH,
    )
    follow_copy.start()
    for s in range(segs):
        for g in inner:
            force(native[s, :, lanes_of(g)], s, g, 0)

    basis_copy.wait()
    chunks = segs * tracers
    half = kry // 2 + 1

    def fold(a):
        return jnp.sum(a, axis=0, keepdims=True)

    def gram(i, acc):
        b = [basis[j, pl.ds(pl.multiple_of(i * rows, rows), rows), :] for j in range(kry)]
        return tuple(acc[m * kry + j] + b[j] * b[(j + m) % kry] for m in range(half) for j in range(kry))

    zero = jnp.zeros((rows, points), jnp.float32)
    sums = lax.fori_loop(0, chunks, gram, (zero,) * (half * kry))
    for m in range(half):
        for j in range(kry):
            part1[me_blk, pl.ds((m + 2) * 8 + j, 1), :] = fold(sums[m * kry + j])

    w_copy.wait()

    def step(slot):
        for s in range(segs):
            came, ahead = halos(s, slot), halos(s, 1 - slot)
            for side, g in enumerate(edges):
                came[1 - side].wait_recv()
                force(move(s, g, slot), s, g, 1 - slot)
                ahead[side].start()
            for h in came:
                h.wait_send()
        for s in range(segs):
            for g in inner:
                force(move(s, g, slot), s, g, 1 - slot)

    def two(i, unused):
        step(0)
        step(1)
        return unused

    lax.fori_loop(0, (STEPS - 1) // 2, two, 0)
    for n in range((STEPS - 1) // 2 * 2, STEPS - 1):
        step(n % 2)
    last = (STEPS - 1) % 2
    for s in range(segs):
        for g in inner:
            native[s, :, lanes_of(g)] = move(s, g, last)
    for s in range(segs):
        for h in halos(s, last):
            h.wait()
        for g in edges:
            native[s, :, lanes_of(g)] = move(s, g, last)
    for s in range(segs):
        for r in range(rows):
            orth_ref[pl.ds(s * per + r, tracers, stride=rows), :] = native[s, :tracers, r * points:(r + 1) * points]
    follow_copy.wait()

    def project(i, acc):
        here = pl.ds(pl.multiple_of(i * rows, rows), rows)
        there = pl.ds(pl.multiple_of(i * rows, rows) + per, rows)
        far = pl.ds(pl.multiple_of(i * rows, rows) + (segs - 1) * per, rows)
        for s in range(segs):
            at = pl.ds(pl.multiple_of(i * rows, rows) + s * per, rows)
            if s < segs - 1:
                nxt = dir_ref[pl.ds(pl.multiple_of(i * rows, rows) + (s + 1) * per, rows), :]
            else:
                nxt = follow[here, :]
            shot = orth_ref[at, :] - nxt
            orth_ref[at, :] = shot
            acc = tuple(acc[j] + basis[j, at, :] * shot for j in range(kry)) + (acc[kry] + shot * shot,)
        return acc

    sums = lax.fori_loop(0, tracers, project, (zero,) * (kry + 1), unroll=4)
    for j in range(kry):
        part1[me_blk, pl.ds(j, 1), :] = fold(sums[j])
    part1[me_blk, pl.ds(8, 8), :] = sums[kry]

    def everyone(part, me, axis, count, sems):
        copies = [
            pltpu.make_async_remote_copy(
                src_ref=part.at[me], dst_ref=part.at[me],
                send_sem=sems.at[0, i - 1], recv_sem=sems.at[1, i - 1],
                device_id={axis: lax.rem(me + i, count)}, device_id_type=MESH,
            )
            for i in range(1, count)
        ]
        for x in copies:
            x.start()
        for x in copies:
            x.wait()
        result = part[0]
        for i in range(1, count):
            result = result + part[i]
        return result

    part2[me_seg] = everyone(part1, me_blk, "blk", n_blk, red_sem1)
    both = everyone(part2, me_seg, "seg", n_seg, red_sem2)
    sumd = jnp.sum(both, axis=1, keepdims=True)
    h = sumd[0:kry]
    hv = [sumd[j:j + 1] for j in range(kry)]
    quad = jnp.zeros((kry, 1), jnp.float32)
    for m in range(half):
        turned = h if m == 0 else jnp.concatenate([h[m:], h[:m]], axis=0)
        weight = 1.0 if m == 0 or 2 * m == kry else 2.0
        quad = quad + weight * (turned * sumd[(m + 2) * 8:(m + 2) * 8 + kry])
    quad = h * (quad - 2.0 * h) + sumd[8:16]
    square = jnp.sum(jnp.broadcast_to(quad, (kry, points)), axis=0, keepdims=True)
    length = jnp.sqrt(jnp.maximum(square, 0.0) / entries)
    coef_ref[kry] = length[0, 0]
    for j in range(kry):
        coef_ref[j] = hv[j][0, 0]
    wide = [jnp.broadcast_to(x, (rows, points)) for x in hv]

    def subtract(i, unused):
        at = pl.ds(pl.multiple_of(i * rows, rows), rows)
        a = hv_sum([wide[j] * basis[j, at, :] for j in range(kry)])
        orth_ref[at, :] = orth_ref[at, :] - a
        return unused

    lax.fori_loop(0, chunks, subtract, 0, unroll=4)


def hv_sum(terms):
    while len(terms) > 1:
        terms = [sum(terms[i:i + 2]) for i in range(0, len(terms), 2)]
    return terms[0]


def on_device(n_seg, n_blk, base_state, direction, coupling, tiles, columns, wet, basis):
    segs, tracers, rows, points = direction.shape
    stored = tiles.shape[2]
    kry = basis.shape[0]
    total = rows * n_blk
    entries = float(segs * n_seg * tracers * total * points)
    pairs = rows // 2
    wide = 2 * REACH + 2
    w = pl.pallas_call(
        functools.partial(merge_kernel, total, rows, stored),
        out_shape=jax.ShapeDtypeStruct((segs, pairs, wide * points, 2 * points), jnp.bfloat16),
        grid_spec=pltpu.PrefetchScalarGridSpec(
            num_scalar_prefetch=1,
            grid=(segs, pairs),
            in_specs=[pl.BlockSpec((1, 2, stored, points, points), lambda s, g, c: (s, g, 0, 0, 0))],
            out_specs=pl.BlockSpec((1, 1, wide * points, 2 * points), lambda s, g, c: (s, g, 0, 0)),
            scratch_shapes=[pltpu.VMEM((2 * wide, points, points), jnp.float32)],
        ),
        compiler_params=pltpu.CompilerParams(vmem_limit_bytes=24 << 20),
        name="merge",
    )(columns.reshape(-1), tiles)
    flat = segs * tracers * rows
    dims = (segs, tracers, rows, points, kry, n_seg, n_blk, entries)
    in_vmem = pl.BlockSpec(memory_space=pltpu.VMEM)
    anywhere = pl.BlockSpec(memory_space=pl.ANY)
    red = (2 + kry // 2 + 1) * 8
    orth, coef = pl.pallas_call(
        functools.partial(steps_kernel, dims),
        out_shape=(
            jax.ShapeDtypeStruct((flat, points), jnp.float32),
            jax.ShapeDtypeStruct((kry + 1,), jnp.float32),
        ),
        in_specs=[in_vmem] * 4 + [anywhere] * 2,
        out_specs=(in_vmem, pl.BlockSpec(memory_space=pltpu.SMEM)),
        scratch_shapes=[
            pltpu.VMEM((segs, pairs, wide * points, 2 * points), jnp.bfloat16),
            pltpu.VMEM((kry, flat, points), jnp.float32),
            pltpu.VMEM((2, segs, PAD, (rows + 2 * REACH) * points), jnp.bfloat16),
            pltpu.VMEM((segs, PAD, rows * points), jnp.float32),
            pltpu.VMEM((PAD, 2 * PAD), jnp.float32),
            pltpu.VMEM((1, rows * points), jnp.float32),
            pltpu.VMEM((tracers * rows, points), jnp.float32),
            pltpu.VMEM((segs, PAD, rows * points), jnp.float32),
            pltpu.VMEM((n_blk, red, points), jnp.float32),
            pltpu.VMEM((n_seg, red, points), jnp.float32),
            pltpu.SemaphoreType.DMA((2, segs, 2)),
            pltpu.SemaphoreType.DMA((2, segs, 2)),
            pltpu.SemaphoreType.DMA((2,)),
            pltpu.SemaphoreType.DMA((2,)),
            pltpu.SemaphoreType.DMA((2, n_blk - 1)),
            pltpu.SemaphoreType.DMA((2, n_seg - 1)),
        ],
        compiler_params=pltpu.CompilerParams(
            collective_id=0, has_side_effects=True, vmem_limit_bytes=40 << 20
        ),
        name="steps",
    )(
        base_state.reshape(flat, points), direction.reshape(flat, points), coupling, wet,
        w, basis.reshape(kry, flat, points),
    )
    return orth.reshape(direction.shape), coef


def solution(mesh):
    in_specs = (
        P(("groups", "seg"), None, "blk", None),
        P(("groups", "seg"), None, "blk", None),
        P("groups", None),
        P("seg", "blk", None, None, None),
        P("seg", "blk", None),
        P("blk", None),
        P(None, ("groups", "seg"), None, "blk", None),
    )
    out_specs = (P(("groups", "seg"), None, "blk", None), P("groups"))
    body = functools.partial(on_device, mesh.shape["seg"], mesh.shape["blk"])
    return jax.shard_map(body, mesh=mesh, in_specs=in_specs, out_specs=out_specs, check_vma=False)
```

profile of v0, /device:TPU:0, one launch (start us, length us, event | category | flops | bytes accessed | tf_op | source)
XLA Modules:
  0.0 76.0 jit_solution(16407406755598619586)
XLA Ops:
  0.6 0.8 %reshape.21.cols_ref = s32[256]{0:T(256)S(1)} reshape(s32[2,8,16]{2,1,0:T(8,128)} %param.11) | data formatting | bytes 2048 | tf_op jit(solution)/shard_map/reshape | solution.py:274
  1.4 0.0 copy-start
  1.4 3.4 %copy-done = bf16[2,8,16,128,128]{4,3,2,1,0:T(8,128)(2,1)S(1)} copy-done((bf16[2,8,16,128,128]{4,3,2,1,0:T(8,128)(2,1)S(1)}, bf16[2,8,16,128,128]{4,3,2,1,0:T(8,128)(2,1)}, u32[]{:S(2)}) %copy-start) | copy-done | bytes 8388632
  4.8 0.0 copy-start.1
  4.8 0.0 copy-start.2
  4.8 0.0 copy-start.3
  4.8 0.0 copy-start.4
  4.8 0.0 copy-start.5
  4.8 5.3 %merge.1.w_hbm = bf16[2,4,768,256]{3,2,1,0:T(8,128)(2,1)S(1)} custom-call(s32[256]{0:T(256)S(1)} %reshape.21.cols_ref, bf16[2,8,16,128,128]{4,3,2,1,0:T(8,128)(2,1)S(1)} %copy-done), custom_call_target="tpu_custom_call" | custom-call | tf_op jit(solution)/shard_map/merge/pallas_call | solution.py:262
  10.2 0.0 copy-done.1
  10.2 0.0 copy-done.2
  10.2 0.0 copy-done.3
  10.2 0.0 copy-done.4
  10.2 0.0 copy-done.5
  10.2 64.6 %steps.1 = (f32[320,128]{1,0:T(8,128)S(1)}, f32[9]{0:T(128)S(1)}) custom-call(f32[320,128]{1,0:T(8,128)S(1)} %bitcast.5, f32[320,128]{1,0:T(8,128)S(1)} %bitcast.6, f32[20,20]{1,0:T(8,128)S(1)} %copy-done.4, s32[8,128]{1,0:T(8,128)S(1)} %copy-done.5, bf16[2,4,768,256]{3,2,1,0:T(8,128)(2,1)S(1)} %merge.1.w_hbm, f32[8,320,128]{2,1,0:T(8,128)S(1)} %bitcast.4), custom_call_target="tpu_custom_call" | custom-call | tf_op jit(solution)/shard_map/steps/pallas_call | solution.py:280
  74.8 0.7 copy.11
  75.5 0.5 copy.12
Async XLA Ops:
  1.4 3.4 %copy-start = (bf16[2,8,16,128,128]{4,3,2,1,0:T(8,128)(2,1)S(1)}, bf16[2,8,16,128,128]{4,3,2,1,0:T(8,128)(2,1)}, u32[]{:S(2)}) copy-start(bf16[2,8,16,128,128]{4,3,2,1,0:T(8,128)(2,1)} %tiles_ref.1) | copy-start | bytes 25165828
  4.8 5.4 %copy-start.1 = (f32[8,2,20,8,128]{4,3,2,1,0:T(8,128)S(1)}, f32[8,2,20,8,128]{4,3,2,1,0:T(8,128)}, u32[]{:S(2)}) copy-start(f32[8,2,20,8,128]{4,3,2,1,0:T(8,128)} %param.13) | copy-start | bytes 3932164
  4.8 5.4 %copy-start.2 = (f32[2,20,8,128]{3,2,1,0:T(8,128)S(1)}, f32[2,20,8,128]{3,2,1,0:T(8,128)}, u32[]{:S(2)}) copy-start(f32[2,20,8,128]{3,2,1,0:T(8,128)} %param.7) | copy-start | bytes 491524
  4.8 5.4 %copy-start.3 = (f32[2,20,8,128]{3,2,1,0:T(8,128)S(1)}, f32[2,20,8,128]{3,2,1,0:T(8,128)}, u32[]{:S(2)}) copy-start(f32[2,20,8,128]{3,2,1,0:T(8,128)} %param.8) | copy-start | bytes 491524
  4.8 5.4 %copy-start.4 = (f32[20,20]{1,0:T(8,128)S(1)}, f32[20,20]{1,0:T(8,128)}, u32[]{:S(2)}) copy-start(f32[20,20]{1,0:T(8,128)} %coup_ref.1) | copy-start | bytes 4804
  4.8 5.4 %copy-start.5 = (s32[8,128]{1,0:T(8,128)S(1)}, s32[8,128]{1,0:T(8,128)}, u32[]{:S(2)}) copy-start(s32[8,128]{1,0:T(8,128)} %wet_ref.1) | copy-start | bytes 12292
where the time goes:
time: 76.2 us; the launch traced here: 76 us
  Pallas kernels  69.9 us (92%)
  local copies, waits for them, and re-layouts  5.36 us (7%)
    pallas_call x1, Pallas kernels, on_device(): pl.pallas_call(functools.partial(steps_kernel, dims), out_shape=(jax.Shap...  64.6 us
    pallas_call x1, Pallas kernels, on_device(): pl.pallas_call(functools.partial(merge_kernel, total, rows, stored), out_...  5.33 us
    unnamed x14, local copies, waits for them, and re-layouts  4.59 us

commit v1 on v0

v1 whole, which is shorter than its diff:
```python
import functools

import jax
import jax.numpy as jnp
from jax import lax
from jax.experimental import pallas as pl
from jax.experimental.pallas import tpu as pltpu
from jax.sharding import PartitionSpec as P

STEPS = 18
MESH = pl.DeviceIdType.MESH
REACH = 2
PAD = 32
BATCH = 4


def merge_kernel(total, rows, stored, cols_ref, tiles_ref, wet_ref, w_ref, acc0, acc1):
    s, g = pl.program_id(0), pl.program_id(1)
    first = lax.axis_index("blk") * rows
    wide = 2 * REACH + 1
    accs = (acc0, acc1)
    for acc in accs:
        acc[...] = jnp.zeros_like(acc)

    def add(k, unused):
        for j in range(2):
            row = 2 * g + j
            col = cols_ref[s, row, k]
            d = lax.rem(col - first - row + (REACH + total), total)
            accs[j][d] += tiles_ref[0, j, k].astype(jnp.float32)
        return unused

    lax.fori_loop(0, stored, add, 0, unroll=4)
    size = acc0.shape[1]
    for j in range(2):
        wet = wet_ref[pl.ds(2 * g + j, 1), :].astype(jnp.float32)
        for c in range(wide + 1):
            d = c - j
            if 0 <= d < wide:
                part = (accs[j][d].T * wet).astype(jnp.bfloat16)
            else:
                part = jnp.zeros((size, size), jnp.bfloat16)
            w_ref[0, 0, c * size:(c + 1) * size, j * size:(j + 1) * size] = part


def steps_kernel(
    dims, base_ref, dir_ref, coup_ref, w, basis, orth_ref, coef_ref,
    drive0, drive1, slope, cc, follow, whalo, shalo, sent, came, part1, part2, gram1, gram2,
    init_send, init_recv, send_sem, recv_sem, follow_sem, red_sem1, red_sem2, gram_sem1, gram_sem2,
):
    segs, tracers, rows, points, kry, n_seg, n_blk, entries = dims
    pairs = rows // 2
    per = tracers * rows
    pair = 2 * points
    drive = (drive0, drive1)
    me_seg, me_blk = lax.axis_index("seg"), lax.axis_index("blk")
    left, right = lax.rem(me_blk + n_blk - 1, n_blk), lax.rem(me_blk + 1, n_blk)

    barrier = pltpu.get_barrier_semaphore()
    for i in range(1, n_blk):
        pl.semaphore_signal(barrier, inc=1, device_id={"blk": lax.rem(me_blk + i, n_blk)}, device_id_type=MESH)
    for i in range(1, n_seg):
        pl.semaphore_signal(barrier, inc=1, device_id={"seg": lax.rem(me_seg + i, n_seg)}, device_id_type=MESH)

    def lanes_of(g, count=1):
        return slice((g + 1) * pair, (g + 1 + count) * pair)

    def dot(a, b):
        return jnp.dot(a, b, preferred_element_type=jnp.float32)

    c = 0.5 * coup_ref[...]
    high = c.astype(jnp.bfloat16)
    low = (c - high.astype(jnp.float32)).astype(jnp.bfloat16)
    cc[...] = jnp.zeros_like(cc)
    cc[:tracers, 0:tracers] = high.astype(jnp.float32)
    cc[:tracers, PAD:PAD + tracers] = low.astype(jnp.float32)
    one = cc[...]
    blank = jnp.zeros_like(one)
    mix = jnp.concatenate(
        [
            jnp.concatenate([one if i == j else blank for j in range(BATCH)], axis=1)
            for i in range(BATCH)
        ],
        axis=0,
    ).astype(jnp.bfloat16)
    slope[...] = jnp.zeros_like(slope)
    for r in range(rows):
        lanes = slice(r * points, (r + 1) * points)
        for s in range(segs):
            t = jnp.tanh(base_ref[pl.ds(s * per + r, tracers, stride=rows), :])
            slope[s, :tracers, lanes] = 1.0 - t * t

    def force(us, ks):
        out = []
        for i in range(0, len(us), BATCH):
            group = us[i:i + BATCH]
            n = len(group)
            xs = [(k * u).astype(jnp.bfloat16) for u, k in zip(group, ks[i:i + BATCH])]
            stack = jnp.concatenate([x for x in xs for unused in range(2)], axis=0)
            added = dot(mix[:n * PAD, :2 * n * PAD], stack)
            out += [(u + added[j * PAD:(j + 1) * PAD]).astype(jnp.bfloat16) for j, u in enumerate(group)]
        return out

    def force_into(units, to):
        values = force([u for u, k, s, g in units], [k for u, k, s, g in units])
        for (u, k, s, g), v in zip(units, values):
            to[s, :, lanes_of(g)] = v

    def slope_of(s, g):
        return slope[s, :, g * pair:(g + 1) * pair]

    def start_of(s, g):
        halves = [
            jnp.concatenate(
                [
                    dir_ref[pl.ds(s * per + 2 * g + j, tracers, stride=rows), :],
                    jnp.zeros((PAD - tracers, points), jnp.float32),
                ],
                axis=0,
            )
            for j in range(2)
        ]
        return jnp.concatenate(halves, axis=1)

    edges = (0, pairs - 1)
    halo = (-1, pairs)

    def initial(i, src, dst, side):
        return pltpu.make_async_remote_copy(
            src_ref=src, dst_ref=dst, send_sem=init_send.at[i], recv_sem=init_recv.at[i],
            device_id={"blk": (left, right)[side]}, device_id_type=MESH,
        )

    first = [
        initial(
            2 * s + side, drive0.at[s, :, lanes_of(edges[side])], drive0.at[s, :, lanes_of(halo[1 - side])], side
        )
        for s in range(segs)
        for side in range(2)
    ]
    slopes = [
        initial(
            2 * segs + 2 * s + side, slope.at[s, :, edges[side] * pair:(edges[side] + 1) * pair],
            shalo.at[1 - side, s], side,
        )
        for s in range(segs)
        for side in range(2)
    ]
    borders = [
        initial(
            4 * segs + 2 * s + side, w.at[s, edges[side], (side * 2) * pair:(side * 2 + 1) * pair, :],
            whalo.at[1 - side, s], side,
        )
        for s in range(segs)
        for side in range(2)
    ]
    force_into([(start_of(s, g), slope_of(s, g), s, g) for s in range(segs) for g in edges], drive0)
    pl.semaphore_wait(barrier, n_blk + n_seg - 2)
    for x in first + slopes + borders:
        x.start()
    follow_copy = pltpu.make_async_remote_copy(
        src_ref=dir_ref.at[0:per], dst_ref=follow, send_sem=follow_sem.at[0], recv_sem=follow_sem.at[1],
        device_id={"seg": lax.rem(me_seg + n_seg - 1, n_seg)}, device_id_type=MESH,
    )
    follow_copy.start()
    inner = range(1, pairs - 1)
    force_into([(start_of(s, g), slope_of(s, g), s, g) for s in range(segs) for g in inner], drive0)

    chunks = segs * tracers
    half = kry // 2 + 1

    def fold(a):
        return jnp.sum(a, axis=0, keepdims=True)

    def everyone(part, me, axis, count, sems):
        return [
            pltpu.make_async_remote_copy(
                src_ref=part.at[me], dst_ref=part.at[me],
                send_sem=sems.at[0, i - 1], recv_sem=sems.at[1, i - 1],
                device_id={axis: lax.rem(me + i, count)}, device_id_type=MESH,
            )
            for i in range(1, count)
        ]

    def total_of(part, copies, count):
        for x in copies:
            x.wait()
        result = part[0]
        for i in range(1, count):
            result = result + part[i]
        return result

    def gram(i, acc):
        b = [basis[j, pl.ds(pl.multiple_of(i * rows, rows), rows), :] for j in range(kry)]
        return tuple(acc[m * kry + j] + b[j] * b[(j + m) % kry] for m in range(half) for j in range(kry))

    zero = jnp.zeros((rows, points), jnp.float32)
    sums = lax.fori_loop(0, chunks, gram, (zero,) * (half * kry))
    for m in range(half):
        for j in range(kry):
            gram1[me_blk, pl.ds(m * 8 + j, 1), :] = fold(sums[m * kry + j])
    gram_copies1 = everyone(gram1, me_blk, "blk", n_blk, gram_sem1)
    for x in gram_copies1:
        x.start()

    def message(n, side):
        return pltpu.make_async_remote_copy(
            src_ref=sent.at[n, side], dst_ref=came.at[n, 1 - side],
            send_sem=send_sem.at[n, side], recv_sem=recv_sem.at[n, 1 - side],
            device_id={"blk": (left, right)[side]}, device_id_type=MESH,
        )

    def arrival(n, side):
        return pltpu.make_async_remote_copy(
            src_ref=sent.at[n, 1 - side], dst_ref=came.at[n, side],
            send_sem=send_sem.at[n, 1 - side], recv_sem=recv_sem.at[n, side],
            device_id={"blk": (left, right)[1 - side]}, device_id_type=MESH,
        )

    def step(n, slot, halos, finish):
        here, there = drive[slot], drive[1 - slot]
        own = [[None, None] for s in range(segs)]
        for s in range(segs):
            own[s][0] = dot(here[s, :, lanes_of(0, 2)], w[s, 0, pair:3 * pair, :])
            own[s][1] = dot(here[s, :, lanes_of(pairs - 2, 2)], w[s, pairs - 1, 0:2 * pair, :])
        if not finish:
            for side in range(2):
                for s in range(segs):
                    sent[n, side, s] = own[s][side].astype(jnp.bfloat16)
            for side in range(2):
                message(n, side).start()
        moved = {}
        for s in range(segs):
            for g in range(1, pairs - 1):
                moved[s, g] = dot(here[s, :, lanes_of(g - 1, 3)], w[s, g])
        if halos:
            mine = [
                [dot(there[s, :, lanes_of(edges[side])], whalo[side, s]) for side in range(2)] for s in range(segs)
            ]
        if not finish:
            force_into([(moved[s, g], slope_of(s, g), s, g) for s in range(segs) for g in inner], there)
        if halos:
            for side in range(2):
                arrival(n - 1, side).wait()
            force_into(
                [
                    (mine[s][side] + came[n - 1, side, s].astype(jnp.float32), shalo[side, s], s, halo[side])
                    for s in range(segs)
                    for side in range(2)
                ],
                here,
            )
        else:
            for x in first:
                x.wait()
        for side in range(2):
            g = edges[side]
            for s in range(segs):
                moved[s, g] = own[s][side] + dot(
                    here[s, :, lanes_of(halo[side])], w[s, g, side * 2 * pair:(side * 2 + 1) * pair, :]
                )
        if finish:
            for s in range(segs):
                for g in range(pairs):
                    for j in range(2):
                        orth_ref[pl.ds(s * per + 2 * g + j, tracers, stride=rows), :] = (
                            moved[s, g][:tracers, j * points:(j + 1) * points]
                        )
        else:
            force_into([(moved[s, g], slope_of(s, g), s, g) for s in range(segs) for g in edges], there)

    step(0, 0, False, False)
    for x in slopes + borders:
        x.wait()

    def two(i, unused):
        step(2 * i + 1, 1, True, False)
        step(2 * i + 2, 0, True, False)
        return unused

    lax.fori_loop(0, (STEPS - 2) // 2, two, 0)
    step(STEPS - 1, 1, True, True)

    gram2[me_seg] = total_of(gram1, gram_copies1, n_blk)
    gram_copies2 = everyone(gram2, me_seg, "seg", n_seg, gram_sem2)
    for x in gram_copies2:
        x.start()
    follow_copy.wait()

    def project(i, acc):
        here = pl.ds(pl.multiple_of(i * rows, rows), rows)
        for s in range(segs):
            at = pl.ds(pl.multiple_of(i * rows, rows) + s * per, rows)
            if s < segs - 1:
                nxt = dir_ref[pl.ds(pl.multiple_of(i * rows, rows) + (s + 1) * per, rows), :]
            else:
                nxt = follow[here, :]
            shot = orth_ref[at, :] - nxt
            orth_ref[at, :] = shot
            acc = tuple(acc[j] + basis[j, at, :] * shot for j in range(kry)) + (acc[kry] + shot * shot,)
        return acc

    sums = lax.fori_loop(0, tracers, project, (zero,) * (kry + 1), unroll=4)
    for j in range(kry):
        part1[me_blk, pl.ds(j, 1), :] = fold(sums[j])
    part1[me_blk, pl.ds(8, 8), :] = sums[kry]

    copies = everyone(part1, me_blk, "blk", n_blk, red_sem1)
    for x in copies:
        x.start()
    part2[me_seg] = total_of(part1, copies, n_blk)
    copies = everyone(part2, me_seg, "seg", n_seg, red_sem2)
    for x in copies:
        x.start()
    gramd = jnp.sum(total_of(gram2, gram_copies2, n_seg), axis=1, keepdims=True)
    sumd = jnp.sum(total_of(part2, copies, n_seg), axis=1, keepdims=True)
    h = sumd[0:kry]
    hv = [sumd[j:j + 1] for j in range(kry)]
    quad = jnp.zeros((kry, 1), jnp.float32)
    for m in range(half):
        turned = h if m == 0 else jnp.concatenate([h[m:], h[:m]], axis=0)
        weight = 1.0 if m == 0 or 2 * m == kry else 2.0
        quad = quad + weight * (turned * gramd[m * 8:m * 8 + kry])
    quad = h * (quad - 2.0 * h) + sumd[8:16]
    square = jnp.sum(jnp.broadcast_to(quad, (kry, points)), axis=0, keepdims=True)
    length = jnp.sqrt(jnp.maximum(square, 0.0) / entries)
    coef_ref[kry] = length[0, 0]
    for j in range(kry):
        coef_ref[j] = hv[j][0, 0]
    wide = [jnp.broadcast_to(x, (rows, points)) for x in hv]

    def subtract(i, unused):
        at = pl.ds(pl.multiple_of(i * rows, rows), rows)
        a = hv_sum([wide[j] * basis[j, at, :] for j in range(kry)])
        orth_ref[at, :] = orth_ref[at, :] - a
        return unused

    lax.fori_loop(0, chunks, subtract, 0, unroll=4)


def hv_sum(terms):
    while len(terms) > 1:
        terms = [sum(terms[i:i + 2]) for i in range(0, len(terms), 2)]
    return terms[0]


def on_device(n_seg, n_blk, base_state, direction, coupling, tiles, columns, wet, basis):
    segs, tracers, rows, points = direction.shape
    stored = tiles.shape[2]
    kry = basis.shape[0]
    total = rows * n_blk
    entries = float(segs * n_seg * tracers * total * points)
    pairs = rows // 2
    pair = 2 * points
    wide = 2 * REACH + 2
    w = pl.pallas_call(
        functools.partial(merge_kernel, total, rows, stored),
        out_shape=jax.ShapeDtypeStruct((segs, pairs, wide * points, 2 * points), jnp.bfloat16),
        grid_spec=pltpu.PrefetchScalarGridSpec(
            num_scalar_prefetch=1,
            grid=(segs, pairs),
            in_specs=[
                pl.BlockSpec((1, 2, stored, points, points), lambda s, g, c: (s, g, 0, 0, 0)),
                pl.BlockSpec((rows, points), lambda s, g, c: (0, 0)),
            ],
            out_specs=pl.BlockSpec((1, 1, wide * points, 2 * points), lambda s, g, c: (s, g, 0, 0)),
            scratch_shapes=[pltpu.VMEM((2 * REACH + 1, points, points), jnp.float32)] * 2,
        ),
        compiler_params=pltpu.CompilerParams(vmem_limit_bytes=48 << 20),
        name="merge",
    )(columns, tiles, wet)
    flat = segs * tracers * rows
    dims = (segs, tracers, rows, points, kry, n_seg, n_blk, entries)
    in_vmem = pl.BlockSpec(memory_space=pltpu.VMEM)
    half = (kry // 2 + 1) * 8
    orth, coef = pl.pallas_call(
        functools.partial(steps_kernel, dims),
        out_shape=(
            jax.ShapeDtypeStruct((flat, points), jnp.float32),
            jax.ShapeDtypeStruct((kry + 1,), jnp.float32),
        ),
        in_specs=[in_vmem] * 5,
        out_specs=(in_vmem, pl.BlockSpec(memory_space=pltpu.SMEM)),
        scratch_shapes=[
            pltpu.VMEM((segs, PAD, (pairs + 2) * pair), jnp.bfloat16),
            pltpu.VMEM((segs, PAD, (pairs + 2) * pair), jnp.bfloat16),
            pltpu.VMEM((segs, PAD, rows * points), jnp.float32),
            pltpu.VMEM((PAD, 2 * PAD), jnp.float32),
            pltpu.VMEM((tracers * rows, points), jnp.float32),
            pltpu.VMEM((2, segs, pair, pair), jnp.bfloat16),
            pltpu.VMEM((2, segs, PAD, pair), jnp.float32),
            pltpu.VMEM((STEPS - 1, 2, segs, PAD, pair), jnp.bfloat16),
            pltpu.VMEM((STEPS - 1, 2, segs, PAD, pair), jnp.bfloat16),
            pltpu.VMEM((n_blk, 16, points), jnp.float32),
            pltpu.VMEM((n_seg, 16, points), jnp.float32),
            pltpu.VMEM((n_blk, half, points), jnp.float32),
            pltpu.VMEM((n_seg, half, points), jnp.float32),
            pltpu.SemaphoreType.DMA((6 * segs,)),
            pltpu.SemaphoreType.DMA((6 * segs,)),
            pltpu.SemaphoreType.DMA((STEPS - 1, 2)),
            pltpu.SemaphoreType.DMA((STEPS - 1, 2)),
            pltpu.SemaphoreType.DMA((2,)),
            pltpu.SemaphoreType.DMA((2, n_blk - 1)),
            pltpu.SemaphoreType.DMA((2, n_seg - 1)),
            pltpu.SemaphoreType.DMA((2, n_blk - 1)),
            pltpu.SemaphoreType.DMA((2, n_seg - 1)),
        ],
        compiler_params=pltpu.CompilerParams(
            collective_id=0, has_side_effects=True, vmem_limit_bytes=40 << 20
        ),
        name="steps",
    )(
        base_state.reshape(flat, points), direction.reshape(flat, points), coupling,
        w, basis.reshape(kry, flat, points),
    )
    return orth.reshape(direction.shape), coef


def solution(mesh):
    in_specs = (
        P(("groups", "seg"), None, "blk", None),
        P(("groups", "seg"), None, "blk", None),
        P("groups", None),
        P("seg", "blk", None, None, None),
        P("seg", "blk", None),
        P("blk", None),
        P(None, ("groups", "seg"), None, "blk", None),
    )
    out_specs = (P(("groups", "seg"), None, "blk", None), P("groups"))
    body = functools.partial(on_device, mesh.shape["seg"], mesh.shape["blk"])
    return jax.shard_map(body, mesh=mesh, in_specs=in_specs, out_specs=out_specs, check_vma=False)
```

time: 76.2 us -> 64 us (0.84)
  Pallas kernels: 69.9 us -> 60.4 us
  local copies, waits for them, and re-layouts: 5.36 us -> 2.57 us
    pallas_call x1, Pallas kernels: 64.6 us -> 52 us  [on_device(): pl.pallas_call(functools.partial(steps_kernel, dims), out_shape=(jax.Shap...]
    pallas_call x1, Pallas kernels: 5.33 us -> 8.41 us  [on_device(): pl.pallas_call(functools.partial(merge_kernel, total, rows, stored), out_...]
    unnamed x14, local copies, waits for them, and re-layouts: 4.59 us -> 2.57 us
    reshape x1 -> x0, local copies, waits for them, and re-layouts: 0.78 us -> none  [on_device(): columns.reshape(-1)]
where the time goes in v1:
time: 64 us; the launch traced here: 63.7 us
  Pallas kernels  60.4 us (94%)
  local copies, waits for them, and re-layouts  2.57 us (4%)
  between operations  0.69 us (1%)
    pallas_call x1, Pallas kernels, on_device(): pl.pallas_call(functools.partial(steps_kernel, dims), out_shape=(jax.Shap...  52 us
    pallas_call x1, Pallas kernels, on_device(): pl.pallas_call(functools.partial(merge_kernel, total, rows, stored), out_...  8.41 us
    unnamed x14, local copies, waits for them, and re-layouts  2.57 us

profile of v1, /device:TPU:0, one launch (start us, length us, event | category | flops | bytes accessed | tf_op | source)
XLA Modules:
  0.0 63.7 jit_solution(11515507869277529902)
XLA Ops:
  0.6 0.0 copy-start.4
  0.6 0.7 %copy-done.4 = s32[2,8,16]{2,1,0:T(8,128)S(1)} copy-done((s32[2,8,16]{2,1,0:T(8,128)S(1)}, s32[2,8,16]{2,1,0:T(8,128)}, u32[]{:S(2)}) %copy-start.4) | copy-done | bytes 1048
  1.3 0.0 copy-start.5
  1.3 0.7 %copy-done.5 = s32[8,128]{1,0:T(8,128)S(1)} copy-done((s32[8,128]{1,0:T(8,128)S(1)}, s32[8,128]{1,0:T(8,128)}, u32[]{:S(2)}) %copy-start.5) | copy-done | bytes 4120
  2.0 0.0 copy-start
  2.0 0.0 copy-start.1
  2.0 0.0 copy-start.2
  2.0 0.0 copy-start.3
  2.0 8.4 %merge.1.w = bf16[2,4,768,256]{3,2,1,0:T(8,128)(2,1)S(1)} custom-call(s32[2,8,16]{2,1,0:T(8,128)S(1)} %copy-done.4, bf16[2,8,16,128,128]{4,3,2,1,0:T(8,128)(2,1)} %tiles_ref.1, s32[8,128]{1,0:T(8,128)S(1)} %copy-done.5), custom_call_target="tpu_custom_call" | custom-call | tf_op jit(solution)/shard_map/merge/pallas_call | solution.py:356
  10.4 0.0 copy-done
  10.5 0.0 copy-done.1
  10.5 0.0 copy-done.2
  10.5 0.0 copy-done.3
  10.5 52.0 %steps.1 = (f32[320,128]{1,0:T(8,128)S(1)}, f32[9]{0:T(128)S(1)}) custom-call(f32[320,128]{1,0:T(8,128)S(1)} %bitcast.5, f32[320,128]{1,0:T(8,128)S(1)} %bitcast.6, f32[20,20]{1,0:T(8,128)S(1)} %copy-done.3, bf16[2,4,768,256]{3,2,1,0:T(8,128)(2,1)S(1)} %merge.1.w, f32[8,320,128]{2,1,0:T(8,128)S(1)} %bitcast.4), custom_call_target="tpu_custom_call" | custom-call | tf_op jit(solution)/shard_map/steps/pallas_call | solution.py:376
  62.5 0.7 %copy.11 = f32[2,20,8,128]{3,2,1,0:T(8,128)} copy(f32[2,20,8,128]{3,2,1,0:T(8,128)S(1)} %bitcast.7) | data formatting | bytes 327680
  63.2 0.5 copy.12
Async XLA Ops:
  0.6 0.7 %copy-start.4 = (s32[2,8,16]{2,1,0:T(8,128)S(1)}, s32[2,8,16]{2,1,0:T(8,128)}, u32[]{:S(2)}) copy-start(s32[2,8,16]{2,1,0:T(8,128)} %cols_ref.1) | copy-start | bytes 3076
  1.3 0.7 %copy-start.5 = (s32[8,128]{1,0:T(8,128)S(1)}, s32[8,128]{1,0:T(8,128)}, u32[]{:S(2)}) copy-start(s32[8,128]{1,0:T(8,128)} %wet_ref.1) | copy-start | bytes 12292
  2.0 8.4 %copy-start = (f32[8,2,20,8,128]{4,3,2,1,0:T(8,128)S(1)}, f32[8,2,20,8,128]{4,3,2,1,0:T(8,128)}, u32[]{:S(2)}) copy-start(f32[8,2,20,8,128]{4,3,2,1,0:T(8,128)} %param.13) | copy-start | bytes 3932164
  2.0 8.4 %copy-start.1 = (f32[2,20,8,128]{3,2,1,0:T(8,128)S(1)}, f32[2,20,8,128]{3,2,1,0:T(8,128)}, u32[]{:S(2)}) copy-start(f32[2,20,8,128]{3,2,1,0:T(8,128)} %param.7) | copy-start | bytes 491524
  2.0 8.4 %copy-start.2 = (f32[2,20,8,128]{3,2,1,0:T(8,128)S(1)}, f32[2,20,8,128]{3,2,1,0:T(8,128)}, u32[]{:S(2)}) copy-start(f32[2,20,8,128]{3,2,1,0:T(8,128)} %param.8) | copy-start | bytes 491524
  2.0 8.5 %copy-start.3 = (f32[20,20]{1,0:T(8,128)S(1)}, f32[20,20]{1,0:T(8,128)}, u32[]{:S(2)}) copy-start(f32[20,20]{1,0:T(8,128)} %coup_ref.1) | copy-start | bytes 4804

commit v2 on v1

v2 whole, which is shorter than its diff:
```python
import functools

import jax
import jax.numpy as jnp
from jax import lax
from jax.experimental import pallas as pl
from jax.experimental.pallas import tpu as pltpu
from jax.sharding import PartitionSpec as P

STEPS = 18
MESH = pl.DeviceIdType.MESH
REACH = 2
PAD = 32
BATCH = 4
BORDER = (((0, 0), (1, 0), (1, 1)), ((0, 0), (0, 1), (1, 1)))


def merge_pair(total, first, stored, row, cols_at, tile_at, wet, accs, put):
    wide = 2 * REACH + 1
    for acc in accs:
        acc[...] = jnp.zeros_like(acc)

    def add(k, unused):
        for j in range(2):
            col = cols_at(row + j, k)
            d = lax.rem(col - first - row - j + (REACH + total), total)
            accs[j][d] += tile_at(j, k).astype(jnp.float32)
        return unused

    lax.fori_loop(0, stored, add, 0, unroll=4)
    size = accs[0].shape[1]
    for j in range(2):
        mask = wet(row + j).astype(jnp.float32)
        for c in range(wide + 1):
            d = c - j
            if 0 <= d < wide:
                put(c, j, (accs[j][d].T * mask).astype(jnp.bfloat16))
            else:
                put(c, j, jnp.zeros((size, size), jnp.bfloat16))


def merge_pairs(total, rows, groups, cols, wet_v, tile_buf, waits, accs, w_ref, then=None):
    first = lax.axis_index("blk") * rows
    segs = cols.shape[0]
    size = accs[0].shape[1]
    for i, g in enumerate(groups):
        for s in range(segs):
            for x in waits[i * segs + s]:
                x.wait()

            def put(c, j, part):
                w_ref[s, i, c * size:(c + 1) * size, j * size:(j + 1) * size] = part

            merge_pair(
                total, first, cols.shape[2], 2 * g, lambda row, k: cols[s, row, k],
                lambda j, k: tile_buf[s, 2 * i + j, k],
                lambda row: wet_v[pl.ds(row, 1), :], accs, put,
            )
            if then is not None:
                then(i, s)


def start_fetches(groups, cols_ref, wet_ref, tiles_ref, cols, wet_v, tile_buf, small_sem, tile_sem):
    small = [
        pltpu.make_async_copy(cols_ref, cols, small_sem.at[0]),
        pltpu.make_async_copy(wet_ref, wet_v, small_sem.at[1]),
    ]
    waits = []
    for i, g in enumerate(groups):
        for s in range(cols_ref.shape[0]):
            waits.append(
                [
                    pltpu.make_async_copy(
                        tiles_ref.at[s, 2 * g + j], tile_buf.at[s, 2 * i + j], tile_sem.at[s, 2 * i + j]
                    )
                    for j in range(2)
                ]
            )
    for x in small:
        x.start()
    for both in waits:
        for x in both:
            x.start()
    return small, waits


def mix_of(coup_ref, cc):
    tracers = coup_ref.shape[0]
    c = 0.5 * coup_ref[...]
    high = c.astype(jnp.bfloat16)
    low = (c - high.astype(jnp.float32)).astype(jnp.bfloat16)
    cc[...] = jnp.zeros_like(cc)
    cc[:tracers, 0:tracers] = high.astype(jnp.float32)
    cc[:tracers, PAD:PAD + tracers] = low.astype(jnp.float32)
    one = cc[...]
    blank = jnp.zeros_like(one)
    return jnp.concatenate(
        [
            jnp.concatenate([one if i == j else blank for j in range(BATCH)], axis=1)
            for i in range(BATCH)
        ],
        axis=0,
    ).astype(jnp.bfloat16)


def dot(a, b):
    return jnp.dot(a, b, preferred_element_type=jnp.float32)


def forced(mix, us, ks):
    out = []
    for i in range(0, len(us), BATCH):
        group = us[i:i + BATCH]
        n = len(group)
        xs = [(k * u).astype(jnp.bfloat16) for u, k in zip(group, ks[i:i + BATCH])]
        stack = jnp.concatenate([x for x in xs for unused in range(2)], axis=0)
        added = dot(mix[:n * PAD, :2 * n * PAD], stack)
        out += [(u + added[j * PAD:(j + 1) * PAD]).astype(jnp.bfloat16) for j, u in enumerate(group)]
    return out


def edge_kernel(
    dims, base_hbm, dir_hbm, coup_hbm, cols_ref, wet_ref, tiles_ref, w_ref, slope_ref, drive_ref, left_ref, right_ref,
    cols, wet_v, tile_buf, acc0, acc1, cc, base, direction, coup, w_v, slope_v, drive_v, out_v,
    small_sem, tile_sem, in_sem, w_sem, out_sem,
):
    segs, tracers, rows, points, total = dims
    pairs = rows // 2
    per = tracers * rows
    pair = 2 * points
    edges = (0, pairs - 1)
    fetches = [
        pltpu.make_async_copy(a, b, in_sem.at[i])
        for i, (a, b) in enumerate([(base_hbm, base), (dir_hbm, direction), (coup_hbm, coup)])
    ]
    for x in fetches:
        x.start()
    small, waits = start_fetches(edges, cols_ref, wet_ref, tiles_ref, cols, wet_v, tile_buf, small_sem, tile_sem)
    for x in fetches:
        x.wait()
    mix = mix_of(coup, cc)

    def native(ref, s, g):
        halves = [
            jnp.concatenate(
                [
                    ref[pl.ds(s * per + 2 * g + j, tracers, stride=rows), :],
                    jnp.zeros((PAD - tracers, points), jnp.float32),
                ],
                axis=0,
            )
            for j in range(2)
        ]
        return jnp.concatenate(halves, axis=1)

    units = [(s, g) for s in range(segs) for g in range(pairs)]
    slopes, starts = [], []
    for s, g in units:
        t = jnp.tanh(native(base, s, g))
        k = 1.0 - t * t
        slope_v[s, :, g * pair:(g + 1) * pair] = k
        slopes.append(k)
        starts.append(native(direction, s, g))
    drives = forced(mix, starts, slopes)
    for (s, g), d, k in zip(units, drives, slopes):
        drive_v[s, :, g * pair:(g + 1) * pair] = d
        if g in edges:
            high = k.astype(jnp.bfloat16)
            low = (k - high.astype(jnp.float32)).astype(jnp.bfloat16)
            for i, x in enumerate((d, high, low)):
                for j in range(2):
                    at = 3 * points + (2 * i + j) * PAD
                    out_v[edges.index(g), s, at:at + PAD, :] = x[:, j * points:(j + 1) * points]
    for x in small:
        x.wait()
    outs = [
        pltpu.make_async_copy(slope_v, slope_ref, out_sem.at[0]),
        pltpu.make_async_copy(drive_v, drive_ref, out_sem.at[1]),
    ]
    for x in outs:
        x.start()

    def merged(i, s):
        for n, (c, j) in enumerate(BORDER[i]):
            c = c + i * 2 * REACH
            out_v[i, s, n * points:(n + 1) * points, :] = (
                w_v[s, i, c * points:(c + 1) * points, j * points:(j + 1) * points]
            )
        copy = pltpu.make_async_copy(w_v.at[s, i], w_ref.at[s, i], w_sem.at[s, i])
        copy.start()
        outs.append(copy)
        if s == segs - 1:
            copy = pltpu.make_async_copy(out_v.at[i], (left_ref, right_ref)[i], out_sem.at[2 + i])
            copy.start()
            outs.append(copy)

    merge_pairs(total, rows, edges, cols, wet_v, tile_buf, waits, (acc0, acc1), w_v, merged)
    for x in outs:
        x.wait()


def inner_kernel(
    dims, basis, cols_ref, wet_ref, tiles_ref, w_ref, gram_ref,
    cols, wet_v, tile_buf, acc0, acc1, small_sem, tile_sem,
):
    segs, tracers, rows, points, total = dims
    pairs = rows // 2
    kry = basis.shape[0]
    groups = tuple(range(1, pairs - 1))
    small, waits = start_fetches(groups, cols_ref, wet_ref, tiles_ref, cols, wet_v, tile_buf, small_sem, tile_sem)
    half = kry // 2 + 1

    def gram(i, acc):
        b = [basis[j, pl.ds(pl.multiple_of(i * rows, rows), rows), :] for j in range(kry)]
        return tuple(acc[m * kry + j] + b[j] * b[(j + m) % kry] for m in range(half) for j in range(kry))

    zero = jnp.zeros((rows, points), jnp.float32)
    sums = lax.fori_loop(0, segs * tracers, gram, (zero,) * (half * kry))
    for m in range(half):
        for j in range(kry):
            gram_ref[pl.ds(m * 8 + j, 1), :] = jnp.sum(sums[m * kry + j], axis=0, keepdims=True)
    for x in small:
        x.wait()
    merge_pairs(total, rows, groups, cols, wet_v, tile_buf, waits, (acc0, acc1), w_ref)


def steps_kernel(
    dims, slope, start, dir_ref, coup_ref, w_edge, w_inner, from_left, from_right, gram_in, basis, orth_ref, coef_ref,
    drive0, drive1, cc, follow, whalo, sent, came, part1, part2, gram1, gram2,
    send_sem, recv_sem, follow_sem, red_sem1, red_sem2, gram_sem1, gram_sem2,
):
    segs, tracers, rows, points, kry, n_seg, n_blk, entries = dims
    pairs = rows // 2
    per = tracers * rows
    pair = 2 * points
    drive = (drive0, drive1)
    me_seg, me_blk = lax.axis_index("seg"), lax.axis_index("blk")
    left, right = lax.rem(me_blk + n_blk - 1, n_blk), lax.rem(me_blk + 1, n_blk)

    barrier = pltpu.get_barrier_semaphore()
    for i in range(1, n_blk):
        pl.semaphore_signal(barrier, inc=1, device_id={"blk": lax.rem(me_blk + i, n_blk)}, device_id_type=MESH)
    for i in range(1, n_seg):
        pl.semaphore_signal(barrier, inc=1, device_id={"seg": lax.rem(me_seg + i, n_seg)}, device_id_type=MESH)

    def lanes_of(g, count=1):
        return slice((g + 1) * pair, (g + 1 + count) * pair)

    mix = mix_of(coup_ref, cc)
    halos_in = (from_left, from_right)

    def force_into(units, to):
        values = forced(mix, [u for u, k, s, g in units], [k for u, k, s, g in units])
        for (u, k, s, g), v in zip(units, values):
            to[s, :, lanes_of(g)] = v

    def slope_of(s, g):
        return slope[s, :, g * pair:(g + 1) * pair]

    def beyond(s, side, i):
        at = 3 * points + 2 * i * PAD
        ref = halos_in[side]
        return jnp.concatenate([ref[s, at:at + PAD, :], ref[s, at + PAD:at + 2 * PAD, :]], axis=1)

    def slope_beyond(s, side):
        return beyond(s, side, 1).astype(jnp.float32) + beyond(s, side, 2).astype(jnp.float32)

    edges = (0, pairs - 1)
    inner = range(1, pairs - 1)
    halo = (-1, pairs)
    for s in range(segs):
        drive0[s, :, pair:(pairs + 1) * pair] = start[s]
        for side in range(2):
            drive0[s, :, lanes_of(halo[side])] = beyond(s, side, 0)
            whalo[side, s] = jnp.zeros((pair, pair), jnp.bfloat16)
            for n, (c, j) in enumerate(BORDER[1 - side]):
                whalo[side, s, c * points:(c + 1) * points, j * points:(j + 1) * points] = (
                    halos_in[side][s, n * points:(n + 1) * points, :]
                )
    gram1[me_blk] = gram_in[...]
    follow_copy = pltpu.make_async_remote_copy(
        src_ref=dir_ref.at[0:per], dst_ref=follow, send_sem=follow_sem.at[0], recv_sem=follow_sem.at[1],
        device_id={"seg": lax.rem(me_seg + n_seg - 1, n_seg)}, device_id_type=MESH,
    )
    chunks = segs * tracers
    half = kry // 2 + 1

    def fold(a):
        return jnp.sum(a, axis=0, keepdims=True)

    def everyone(part, me, axis, count, sems):
        return [
            pltpu.make_async_remote_copy(
                src_ref=part.at[me], dst_ref=part.at[me],
                send_sem=sems.at[0, i - 1], recv_sem=sems.at[1, i - 1],
                device_id={axis: lax.rem(me + i, count)}, device_id_type=MESH,
            )
            for i in range(1, count)
        ]

    def total_of(part, copies, count):
        for x in copies:
            x.wait()
        result = part[0]
        for i in range(1, count):
            result = result + part[i]
        return result

    zero = jnp.zeros((rows, points), jnp.float32)
    gram_copies1 = everyone(gram1, me_blk, "blk", n_blk, gram_sem1)

    def message(n, side):
        return pltpu.make_async_remote_copy(
            src_ref=sent.at[n, side], dst_ref=came.at[n, 1 - side],
            send_sem=send_sem.at[n, side], recv_sem=recv_sem.at[n, 1 - side],
            device_id={"blk": (left, right)[side]}, device_id_type=MESH,
        )

    def arrival(n, side):
        return pltpu.make_async_remote_copy(
            src_ref=sent.at[n, 1 - side], dst_ref=came.at[n, side],
            send_sem=send_sem.at[n, 1 - side], recv_sem=recv_sem.at[n, side],
            device_id={"blk": (left, right)[1 - side]}, device_id_type=MESH,
        )

    def step(n, slot, halos, finish):
        here, there = drive[slot], drive[1 - slot]
        own = [[None, None] for s in range(segs)]
        for s in range(segs):
            own[s][0] = dot(here[s, :, lanes_of(0, 2)], w_edge[s, 0, pair:3 * pair, :])
            own[s][1] = dot(here[s, :, lanes_of(pairs - 2, 2)], w_edge[s, 1, 0:2 * pair, :])
        def send():
            for side in range(2):
                for s in range(segs):
                    sent[n, side, s] = own[s][side].astype(jnp.bfloat16)
            if not halos:
                pl.semaphore_wait(barrier, n_blk + n_seg - 2)
            for side in range(2):
                message(n, side).start()

        if halos and not finish:
            send()
        moved = {}
        for s in range(segs):
            for g in range(1, pairs - 1):
                moved[s, g] = dot(here[s, :, lanes_of(g - 1, 3)], w_inner[s, g - 1])
        if halos:
            mine = [
                [dot(there[s, :, lanes_of(edges[side])], whalo[side, s]) for side in range(2)]
                for s in range(segs)
            ]
        if not finish:
            force_into([(moved[s, g], slope_of(s, g), s, g) for s in range(segs) for g in inner], there)
        if not halos:
            send()
        if halos:
            for side in range(2):
                arrival(n - 1, side).wait()
            force_into(
                [
                    (mine[s][side] + came[n - 1, side, s].astype(jnp.float32), slope_beyond(s, side), s, halo[side])
                    for s in range(segs)
                    for side in range(2)
                ],
                here,
            )
        for side in range(2):
            g = edges[side]
            for s in range(segs):
                moved[s, g] = own[s][side] + dot(
                    here[s, :, lanes_of(halo[side])], w_edge[s, side, side * 2 * pair:(side * 2 + 1) * pair, :]
                )
        if finish:
            for s in range(segs):
                for g in range(pairs):
                    for j in range(2):
                        orth_ref[pl.ds(s * per + 2 * g + j, tracers, stride=rows), :] = (
                            moved[s, g][:tracers, j * points:(j + 1) * points]
                        )
        else:
            force_into([(moved[s, g], slope_of(s, g), s, g) for s in range(segs) for g in edges], there)

    step(0, 0, False, False)
    follow_copy.start()
    for x in gram_copies1:
        x.start()

    def two(i, unused):
        step(2 * i + 1, 1, True, False)
        step(2 * i + 2, 0, True, False)
        return unused

    lax.fori_loop(0, (STEPS - 2) // 2, two, 0)
    step(STEPS - 1, 1, True, True)

    gram2[me_seg] = total_of(gram1, gram_copies1, n_blk)
    gram_copies2 = everyone(gram2, me_seg, "seg", n_seg, gram_sem2)
    for x in gram_copies2:
        x.start()
    follow_copy.wait()

    def project(i, acc):
        here = pl.ds(pl.multiple_of(i * rows, rows), rows)
        for s in range(segs):
            at = pl.ds(pl.multiple_of(i * rows, rows) + s * per, rows)
            if s < segs - 1:
                nxt = dir_ref[pl.ds(pl.multiple_of(i * rows, rows) + (s + 1) * per, rows), :]
            else:
                nxt = follow[here, :]
            shot = orth_ref[at, :] - nxt
            orth_ref[at, :] = shot
            acc = tuple(acc[j] + basis[j, at, :] * shot for j in range(kry)) + (acc[kry] + shot * shot,)
        return acc

    sums = lax.fori_loop(0, tracers, project, (zero,) * (kry + 1), unroll=4)
    for j in range(kry):
        part1[me_blk, pl.ds(j, 1), :] = fold(sums[j])
    part1[me_blk, pl.ds(8, 8), :] = sums[kry]

    copies = everyone(part1, me_blk, "blk", n_blk, red_sem1)
    for x in copies:
        x.start()
    part2[me_seg] = total_of(part1, copies, n_blk)
    copies = everyone(part2, me_seg, "seg", n_seg, red_sem2)
    for x in copies:
        x.start()
    gramd = jnp.sum(total_of(gram2, gram_copies2, n_seg), axis=1, keepdims=True)
    sumd = jnp.sum(total_of(part2, copies, n_seg), axis=1, keepdims=True)
    h = sumd[0:kry]
    hv = [sumd[j:j + 1] for j in range(kry)]
    quad = jnp.zeros((kry, 1), jnp.float32)
    for m in range(half):
        turned = h if m == 0 else jnp.concatenate([h[m:], h[:m]], axis=0)
        weight = 1.0 if m == 0 or 2 * m == kry else 2.0
        quad = quad + weight * (turned * gramd[m * 8:m * 8 + kry])
    quad = h * (quad - 2.0 * h) + sumd[8:16]
    square = jnp.sum(jnp.broadcast_to(quad, (kry, points)), axis=0, keepdims=True)
    length = jnp.sqrt(jnp.maximum(square, 0.0) / entries)
    coef_ref[kry] = length[0, 0]
    for j in range(kry):
        coef_ref[j] = hv[j][0, 0]
    wide = [jnp.broadcast_to(x, (rows, points)) for x in hv]

    def subtract(i, unused):
        at = pl.ds(pl.multiple_of(i * rows, rows), rows)
        a = hv_sum([wide[j] * basis[j, at, :] for j in range(kry)])
        orth_ref[at, :] = orth_ref[at, :] - a
        return unused

    lax.fori_loop(0, chunks, subtract, 0, unroll=4)


def hv_sum(terms):
    while len(terms) > 1:
        terms = [sum(terms[i:i + 2]) for i in range(0, len(terms), 2)]
    return terms[0]


def on_device(n_seg, n_blk, base_state, direction, coupling, tiles, columns, wet, basis):
    segs, tracers, rows, points = direction.shape
    stored = tiles.shape[2]
    kry = basis.shape[0]
    total = rows * n_blk
    entries = float(segs * n_seg * tracers * total * points)
    pairs = rows // 2
    pair = 2 * points
    wide = 2 * REACH + 2
    flat = segs * tracers * rows
    base_flat = base_state.reshape(flat, points)
    dir_flat = direction.reshape(flat, points)
    basis_flat = basis.reshape(kry, flat, points)
    in_vmem = pl.BlockSpec(memory_space=pltpu.VMEM)
    in_hbm = pl.BlockSpec(memory_space=pltpu.HBM)
    bf16, f32 = jnp.bfloat16, jnp.float32
    shape = jax.ShapeDtypeStruct

    def scratch_of(count):
        return [
            pltpu.SMEM((segs, rows, stored), jnp.int32),
            pltpu.VMEM((rows, points), jnp.int32),
            pltpu.VMEM((segs, 2 * count, stored, points, points), bf16),
            pltpu.VMEM((2 * REACH + 1, points, points), f32),
            pltpu.VMEM((2 * REACH + 1, points, points), f32),
        ]

    def sems_of(count):
        return [pltpu.SemaphoreType.DMA((2,)), pltpu.SemaphoreType.DMA((segs, 2 * count))]

    dims = (segs, tracers, rows, points, total)
    work = segs * rows * stored * points * points
    border = shape((segs, 3 * points + 6 * PAD, points), bf16)
    w_edge, slope, start, to_left, to_right = pl.pallas_call(
        functools.partial(edge_kernel, dims),
        out_shape=(
            shape((segs, 2, wide * points, pair), bf16), shape((segs, PAD, rows * points), f32),
            shape((segs, PAD, rows * points), bf16), border, border,
        ),
        in_specs=[in_hbm] * 6,
        out_specs=(in_hbm,) * 5,
        scratch_shapes=scratch_of(2) + [
            pltpu.VMEM((PAD, 2 * PAD), f32),
            pltpu.VMEM((flat, points), f32),
            pltpu.VMEM((flat, points), f32),
            pltpu.VMEM((tracers, tracers), f32),
            pltpu.VMEM((segs, 2, wide * points, pair), bf16),
            pltpu.VMEM((segs, PAD, rows * points), f32),
            pltpu.VMEM((segs, PAD, rows * points), bf16),
            pltpu.VMEM((2, segs, 3 * points + 6 * PAD, points), bf16),
        ] + sems_of(2) + [
            pltpu.SemaphoreType.DMA((3,)),
            pltpu.SemaphoreType.DMA((segs, 2)),
            pltpu.SemaphoreType.DMA((4,)),
        ],
        compiler_params=pltpu.CompilerParams(vmem_limit_bytes=48 << 20),
        cost_estimate=pl.CostEstimate(flops=8 * work, bytes_accessed=work, transcendentals=0),
        name="edge",
    )(base_flat, dir_flat, coupling, columns, wet, tiles)
    ring = range(n_blk)
    from_right = lax.ppermute(to_left, "blk", [(i, (i + n_blk - 1) % n_blk) for i in ring])
    from_left = lax.ppermute(to_right, "blk", [(i, (i + 1) % n_blk) for i in ring])
    w_inner, gram = pl.pallas_call(
        functools.partial(inner_kernel, dims),
        out_shape=(
            shape((segs, pairs - 2, wide * points, pair), bf16), shape(((kry // 2 + 1) * 8, points), f32),
        ),
        in_specs=[in_vmem] + [in_hbm] * 3,
        out_specs=(in_vmem,) * 2,
        scratch_shapes=scratch_of(pairs - 2) + sems_of(pairs - 2),
        compiler_params=pltpu.CompilerParams(vmem_limit_bytes=48 << 20),
        cost_estimate=pl.CostEstimate(flops=8 * work, bytes_accessed=work, transcendentals=0),
        name="inner",
    )(basis_flat, columns, wet, tiles)
    dims = (segs, tracers, rows, points, kry, n_seg, n_blk, entries)
    half = (kry // 2 + 1) * 8
    orth, coef = pl.pallas_call(
        functools.partial(steps_kernel, dims),
        out_shape=(
            jax.ShapeDtypeStruct((flat, points), jnp.float32),
            jax.ShapeDtypeStruct((kry + 1,), jnp.float32),
        ),
        in_specs=[in_vmem] * 10,
        out_specs=(in_vmem, pl.BlockSpec(memory_space=pltpu.SMEM)),
        scratch_shapes=[
            pltpu.VMEM((segs, PAD, (pairs + 2) * pair), jnp.bfloat16),
            pltpu.VMEM((segs, PAD, (pairs + 2) * pair), jnp.bfloat16),
            pltpu.VMEM((PAD, 2 * PAD), jnp.float32),
            pltpu.VMEM((tracers * rows, points), jnp.float32),
            pltpu.VMEM((2, segs, pair, pair), jnp.bfloat16),
            pltpu.VMEM((STEPS - 1, 2, segs, PAD, pair), jnp.bfloat16),
            pltpu.VMEM((STEPS - 1, 2, segs, PAD, pair), jnp.bfloat16),
            pltpu.VMEM((n_blk, 16, points), jnp.float32),
            pltpu.VMEM((n_seg, 16, points), jnp.float32),
            pltpu.VMEM((n_blk, half, points), jnp.float32),
            pltpu.VMEM((n_seg, half, points), jnp.float32),
            pltpu.SemaphoreType.DMA((STEPS - 1, 2)),
            pltpu.SemaphoreType.DMA((STEPS - 1, 2)),
            pltpu.SemaphoreType.DMA((2,)),
            pltpu.SemaphoreType.DMA((2, n_blk - 1)),
            pltpu.SemaphoreType.DMA((2, n_seg - 1)),
            pltpu.SemaphoreType.DMA((2, n_blk - 1)),
            pltpu.SemaphoreType.DMA((2, n_seg - 1)),
        ],
        compiler_params=pltpu.CompilerParams(
            collective_id=0, has_side_effects=True, vmem_limit_bytes=40 << 20
        ),
        name="steps",
    )(slope, start, dir_flat, coupling, w_edge, w_inner, from_left, from_right, gram, basis_flat)
    return orth.reshape(direction.shape), coef


def solution(mesh):
    in_specs = (
        P(("groups", "seg"), None, "blk", None),
        P(("groups", "seg"), None, "blk", None),
        P("groups", None),
        P("seg", "blk", None, None, None),
        P("seg", "blk", None),
        P("blk", None),
        P(None, ("groups", "seg"), None, "blk", None),
    )
    out_specs = (P(("groups", "seg"), None, "blk", None), P("groups"))
    body = functools.partial(on_device, mesh.shape["seg"], mesh.shape["blk"])
    return jax.shard_map(body, mesh=mesh, in_specs=in_specs, out_specs=out_specs, check_vma=False)
```

time: 64 us -> 63.3 us (0.989)
  Pallas kernels: 60.4 us -> 50.6 us
  waiting for transfers between devices: 0 us -> 4.02 us
  local copies, waits for them, and re-layouts: 2.57 us -> 5.11 us
  starting transfers between devices: 0 us -> 2.52 us
    pallas_call x1, Pallas kernels: 52 us -> 42.6 us  [on_device(): pl.pallas_call(functools.partial(steps_kernel, dims), out_shape=(jax.Shap...]
    ppermute x0 -> x2, waiting for transfers between devices: none -> 4.02 us  [the longest x1 2.48 us: on_device(): lax.ppermute(to_left, 'blk', [(i, (i + n_blk - 1) % n_blk) for i in ring])]
    unnamed x14 -> x20, local copies, waits for them, and re-layouts: 2.57 us -> 5.11 us
    ppermute x0 -> x2, starting transfers between devices: none -> 2.52 us  [the longest x1 2.02 us: on_device(): lax.ppermute(to_left, 'blk', [(i, (i + n_blk - 1) % n_blk) for i in ring])]
    pallas_call x1 -> x2, Pallas kernels: 8.41 us -> 8.02 us  [the longest x1 4.74 us: on_device(): pl.pallas_call(functools.partial(edge_kernel, dims), out_shape=(shape((se...]
  transfers between devices with their start and end apart: 0 -> 2, of which waited for: 0 -> 2; matrix products, arithmetic and copies ran while one was open for 0% -> 0% of each run, Pallas kernels for 0% -> 5%
where the time goes in v2:
time: 63.3 us; the launch traced here: 63 us
  Pallas kernels  50.6 us (80%)
  local copies, waits for them, and re-layouts  5.11 us (8%)
  waiting for transfers between devices  4.02 us (6%)
  starting transfers between devices  2.52 us (4%)
  between operations  0.68 us (1%)
    pallas_call x1, Pallas kernels, on_device(): pl.pallas_call(functools.partial(steps_kernel, dims), out_shape=(jax.Shap...  42.6 us
    unnamed x20, local copies, waits for them, and re-layouts  5.11 us
    pallas_call x1, Pallas kernels, on_device(): pl.pallas_call(functools.partial(edge_kernel, dims), out_shape=(shape((se...  4.74 us
    pallas_call x1, Pallas kernels, on_device(): pl.pallas_call(functools.partial(inner_kernel, dims), out_shape=(shape((s...  3.28 us
    ppermute x1, waiting for transfers between devices, on_device(): lax.ppermute(to_left, 'blk', [(i, (i + n_blk - 1) % n_blk) for i in ring])  2.48 us
    ppermute x1, starting transfers between devices, on_device(): lax.ppermute(to_left, 'blk', [(i, (i + n_blk - 1) % n_blk) for i in ring])  2.02 us
    ppermute x1, waiting for transfers between devices, on_device(): lax.ppermute(to_right, 'blk', [(i, (i + 1) % n_blk) for i in ring])  1.54 us
  transfers between devices with their start and end apart: 2, of which 2 were waited for; matrix products, arithmetic and copies ran while one was open for 0% of the time, Pallas kernels for 5%

profile of v2, /device:TPU:0, one launch (start us, length us, event | category | flops | bytes accessed | tf_op | source)
XLA Modules:
  0.0 63.0 jit_solution(13282766844320623628)
XLA Ops:
  0.6 0.0 copy-start.1
  0.6 0.9 %copy-done.1 = f32[2,20,8,128]{3,2,1,0:T(8,128)S(1)} copy-done((f32[2,20,8,128]{3,2,1,0:T(8,128)S(1)}, f32[2,20,8,128]{3,2,1,0:T(8,128)}, u32[]{:S(2)}) %copy-start.1) | copy-done | bytes 163864
  1.5 0.0 copy-start.3
  1.6 0.9 %copy-done.3 = f32[2,20,8,128]{3,2,1,0:T(8,128)S(1)} copy-done((f32[2,20,8,128]{3,2,1,0:T(8,128)S(1)}, f32[2,20,8,128]{3,2,1,0:T(8,128)}, u32[]{:S(2)}) %copy-start.3) | copy-done | bytes 163864
  2.5 0.0 copy-start.4
  2.5 0.7 %copy-done.4 = f32[20,20]{1,0:T(8,128)S(1)} copy-done((f32[20,20]{1,0:T(8,128)S(1)}, f32[20,20]{1,0:T(8,128)}, u32[]{:S(2)}) %copy-start.4) | copy-done | bytes 1624
  3.2 0.0 copy-start.6
  3.2 0.7 %copy-done.6 = s32[2,8,16]{2,1,0:T(8,128)S(1)} copy-done((s32[2,8,16]{2,1,0:T(8,128)S(1)}, s32[2,8,16]{2,1,0:T(8,128)}, u32[]{:S(2)}) %copy-start.6) | copy-done | bytes 1048
  3.9 0.0 copy-start.8
  3.9 0.7 %copy-done.8 = s32[8,128]{1,0:T(8,128)S(1)} copy-done((s32[8,128]{1,0:T(8,128)S(1)}, s32[8,128]{1,0:T(8,128)}, u32[]{:S(2)}) %copy-start.8) | copy-done | bytes 4120
  4.6 0.0 copy-start
  4.6 4.7 %edge.1 = (bf16[2,2,768,256]{3,2,1,0:T(8,128)(2,1)S(1)}, f32[2,32,1024]{2,1,0:T(8,128)S(1)}, bf16[2,32,1024]{2,1,0:T(8,128)(2,1)S(1)}, bf16[2,576,128]{2,1,0:T(8,128)(2,1)S(1)}, bf16[2,576,128]{2,1,0:T(8,128)(2,1)S(1)}) custom-call(f32[320,128]{1,0:T(8,128)S(1)} %bitcast.9, f32[320,128]{1,0:T(8,128)S(1)} %bitcast.6, f32[20,20]{1,0:T(8,128)S(1)} %copy-done.4, ...), custom_call_target="tpu_custom_call" | custom-call | flops 33554432 | bytes 4194304 | tf_op jit(solution)/shard_map/edge/pallas_call | solution.py:492
  9.3 0.5 collective-permute-start
  9.8 2.0 %collective-permute-start.1 = (bf16[2,576,128]{2,1,0:T(8,128)(2,1)S(1)}, bf16[2,576,128]{2,1,0:T(8,128)(2,1)S(1)}, u32[]{:S(2)}, u32[]{:S(2)}) collective-permute-start(bf16[2,576,128]{2,1,0:T(8,128)(2,1)S(1)} %get-tuple-element.16), channel_id=1, source_target_pairs={{0,3},{1,0},{2,1},{3,2},{4,7},{5,4},{6,5},{7,6},{8,11},{9,8},{10,9... | collective-permute-start | bytes 884744 | tf_op jit(solution)/shard_map/ppermute | solution.py:519
  11.8 0.0 copy-done
  11.8 0.0 copy-done.7
  11.9 3.3 %inner.1 = (bf16[2,2,768,256]{3,2,1,0:T(8,128)(2,1)S(1)}, f32[40,128]{1,0:T(8,128)S(1)}) custom-call(f32[8,320,128]{2,1,0:T(8,128)S(1)} %bitcast.4, s32[2,8,16]{2,1,0:T(8,128)S(1)} %copy-done.7, s32[8,128]{1,0:T(8,128)S(1)} %copy-done.8, bf16[2,8,16,128,128]{4,3,2,1,0:T(8,128)(2,1)} %tiles_ref.3), custom_call_target="tpu_custom_call" | custom-call | flops 33554432 | bytes 4194304 | tf_op jit(solution)/shard_map/inner/pallas_call | solution.py:521
  15.1 1.5 %collective-permute-done.from_left = bf16[2,576,128]{2,1,0:T(8,128)(2,1)S(1)} collective-permute-done((bf16[2,576,128]{2,1,0:T(8,128)(2,1)S(1)}, bf16[2,576,128]{2,1,0:T(8,128)(2,1)S(1)}, u32[]{:S(2)}, u32[]{:S(2)}) %collective-permute-start) | collective-permute-done | bytes 294944 | tf_op jit(solution)/shard_map/ppermute | solution.py:520
  16.7 2.5 %collective-permute-done.1.from_right = bf16[2,576,128]{2,1,0:T(8,128)(2,1)S(1)} collective-permute-done((bf16[2,576,128]{2,1,0:T(8,128)(2,1)S(1)}, bf16[2,576,128]{2,1,0:T(8,128)(2,1)S(1)}, u32[]{:S(2)}, u32[]{:S(2)}) %collective-permute-start.1) | collective-permute-done | bytes 294944 | tf_op jit(solution)/shard_map/ppermute | solution.py:519
  19.2 0.0 copy-done.2
  19.2 0.0 copy-done.5
  19.2 42.6 %steps.1 = (f32[320,128]{1,0:T(8,128)S(1)}, f32[9]{0:T(128)S(1)}) custom-call(f32[2,32,1024]{2,1,0:T(8,128)S(1)} %get-tuple-element.11.slope, bf16[2,32,1024]{2,1,0:T(8,128)(2,1)S(1)} %get-tuple-element.12.start, f32[320,128]{1,0:T(8,128)S(1)} %bitcast.7, f32[20,20]{1,0:T(8,128)S(1)} %copy-done.5, bf16[2,2,768,256]{3,2,1,0:T(8,128)(2,1)S(1)} %get-tuple-element.13.w_edge, ...), custom_call_target="tpu_custom_call" | custom-call | tf_op jit(solution)/shard_map/steps/pallas_call | solution.py:535
  61.8 0.7 %copy.11 = f32[2,20,8,128]{3,2,1,0:T(8,128)} copy(f32[2,20,8,128]{3,2,1,0:T(8,128)S(1)} %bitcast.8) | data formatting | bytes 327680
  62.4 0.5 copy.12
  (3 shorter events, 0.0 us)
Async XLA Ops:
  0.6 0.9 %copy-start.1 = (f32[2,20,8,128]{3,2,1,0:T(8,128)S(1)}, f32[2,20,8,128]{3,2,1,0:T(8,128)}, u32[]{:S(2)}) copy-start(f32[2,20,8,128]{3,2,1,0:T(8,128)} %param.8) | copy-start | bytes 491524
  1.5 0.9 %copy-start.3 = (f32[2,20,8,128]{3,2,1,0:T(8,128)S(1)}, f32[2,20,8,128]{3,2,1,0:T(8,128)}, u32[]{:S(2)}) copy-start(f32[2,20,8,128]{3,2,1,0:T(8,128)} %param.7) | copy-start | bytes 491524
  2.5 0.7 %copy-start.4 = (f32[20,20]{1,0:T(8,128)S(1)}, f32[20,20]{1,0:T(8,128)}, u32[]{:S(2)}) copy-start(f32[20,20]{1,0:T(8,128)} %coup_ref.1) | copy-start | bytes 4804
  3.2 0.7 %copy-start.6 = (s32[2,8,16]{2,1,0:T(8,128)S(1)}, s32[2,8,16]{2,1,0:T(8,128)}, u32[]{:S(2)}) copy-start(s32[2,8,16]{2,1,0:T(8,128)} %cols_ref.3) | copy-start | bytes 3076
  3.9 0.7 %copy-start.8 = (s32[8,128]{1,0:T(8,128)S(1)}, s32[8,128]{1,0:T(8,128)}, u32[]{:S(2)}) copy-start(s32[8,128]{1,0:T(8,128)} %wet_ref.3) | copy-start | bytes 12292
  4.6 7.3 %copy-start = (f32[8,2,20,8,128]{4,3,2,1,0:T(8,128)S(1)}, f32[8,2,20,8,128]{4,3,2,1,0:T(8,128)}, u32[]{:S(2)}) copy-start(f32[8,2,20,8,128]{4,3,2,1,0:T(8,128)} %param.13) | copy-start | bytes 3932164
  4.6 7.3 %copy-start.7 = (s32[2,8,16]{2,1,0:T(8,128)S(1)}, s32[2,8,16]{2,1,0:T(8,128)}, u32[]{:S(2)}) copy-start(s32[2,8,16]{2,1,0:T(8,128)} %cols_ref.3) | copy-start | bytes 3076
  9.3 7.4 %collective-permute-start = (bf16[2,576,128]{2,1,0:T(8,128)(2,1)S(1)}, bf16[2,576,128]{2,1,0:T(8,128)(2,1)S(1)}, u32[]{:S(2)}, u32[]{:S(2)}) collective-permute-start(bf16[2,576,128]{2,1,0:T(8,128)(2,1)S(1)} %get-tuple-element.15), channel_id=1, source_target_pairs={{0,1},{1,2},{2,3},{3,0},{4,5},{5,6},{6,7},{7,4},{8,9},{9,10},{10,1... | collective-permute-start | bytes 884744 | tf_op jit(solution)/shard_map/ppermute | solution.py:520
  9.8 9.3 %collective-permute-start.1 = (bf16[2,576,128]{2,1,0:T(8,128)(2,1)S(1)}, bf16[2,576,128]{2,1,0:T(8,128)(2,1)S(1)}, u32[]{:S(2)}, u32[]{:S(2)}) collective-permute-start(bf16[2,576,128]{2,1,0:T(8,128)(2,1)S(1)} %get-tuple-element.16), channel_id=1, source_target_pairs={{0,3},{1,0},{2,1},{3,2},{4,7},{5,4},{6,5},{7,6},{8,11},{9,8},{10,9... | collective-permute-start | bytes 884744 | tf_op jit(solution)/shard_map/ppermute | solution.py:519
  11.8 7.3 %copy-start.2 = (f32[2,20,8,128]{3,2,1,0:T(8,128)S(1)}, f32[2,20,8,128]{3,2,1,0:T(8,128)}, u32[]{:S(2)}) copy-start(f32[2,20,8,128]{3,2,1,0:T(8,128)} %param.8) | copy-start | bytes 491524
  11.8 7.3 %copy-start.5 = (f32[20,20]{1,0:T(8,128)S(1)}, f32[20,20]{1,0:T(8,128)}, u32[]{:S(2)}) copy-start(f32[20,20]{1,0:T(8,128)} %coup_ref.1) | copy-start | bytes 4804

commit v3 on v2

--- a/solution.py
+++ b/solution.py
@@ -8,6 +8,7 @@
 from jax.sharding import PartitionSpec as P
 
 STEPS = 18
+SWITCH = 5
 MESH = pl.DeviceIdType.MESH
 REACH = 2
 PAD = 32
@@ -226,8 +227,8 @@
 
 def steps_kernel(
     dims, slope, start, dir_ref, coup_ref, w_edge, w_inner, from_left, from_right, gram_in, basis, orth_ref, coef_ref,
-    drive0, drive1, cc, follow, whalo, sent, came, part1, part2, gram1, gram2,
-    send_sem, recv_sem, follow_sem, red_sem1, red_sem2, gram_sem1, gram_sem2,
+    drive0, drive1, cc, follow, whalo, whalo2, hold, sent, came, part1, part2, gram1, gram2,
+    send_sem, recv_sem, border_send, border_recv, follow_sem, red_sem1, red_sem2, gram_sem1, gram_sem2,
 ):
     segs, tracers, rows, points, kry, n_seg, n_blk, entries = dims
     pairs = rows // 2
@@ -323,7 +324,7 @@
             device_id={"blk": (left, right)[1 - side]}, device_id_type=MESH,
         )
 
-    def step(n, slot, halos, finish):
+    def step(n, slot, halos, pieces):
         here, there = drive[slot], drive[1 - slot]
         own = [[None, None] for s in range(segs)]
         for s in range(segs):
@@ -337,8 +338,10 @@
                 pl.semaphore_wait(barrier, n_blk + n_seg - 2)
             for side in range(2):
                 message(n, side).start()
-
-        if halos and not finish:
+            for x in pieces:
+                x.start()
+
+        if halos:
             send()
         moved = {}
         for s in range(segs):
@@ -349,8 +352,7 @@
                 [dot(there[s, :, lanes_of(edges[side])], whalo[side, s]) for side in range(2)]
                 for s in range(segs)
             ]
-        if not finish:
-            force_into([(moved[s, g], slope_of(s, g), s, g) for s in range(segs) for g in inner], there)
+        force_into([(moved[s, g], slope_of(s, g), s, g) for s in range(segs) for g in inner], there)
         if not halos:
             send()
         if halos:
@@ -370,6 +372,53 @@
                 moved[s, g] = own[s][side] + dot(
                     here[s, :, lanes_of(halo[side])], w_edge[s, side, side * 2 * pair:(side * 2 + 1) * pair, :]
                 )
+        force_into([(moved[s, g], slope_of(s, g), s, g) for s in range(segs) for g in edges], there)
+
+    def beside(n, slot):
+        here = drive[slot]
+        for s in range(segs):
+            r = (
+                dot(here[s, :, lanes_of(1)], w_edge[s, 0, 2 * pair:3 * pair, :]),
+                dot(here[s, :, lanes_of(pairs - 2)], w_edge[s, 1, 0:pair, :]),
+            )
+            for side in range(2):
+                hold[slot, s, side] = r[side]
+                sent[n, side, s] = r[side].astype(jnp.bfloat16)
+        for side in range(2):
+            message(n, side).start()
+
+    def late_step(n, slot, finish):
+        here, there = drive[slot], drive[1 - slot]
+        moved = {}
+        for s in range(segs):
+            for g in inner:
+                moved[s, g] = dot(here[s, :, lanes_of(g - 1, 3)], w_inner[s, g - 1])
+        mine = {}
+        for s in range(segs):
+            for side in range(2):
+                old = dot(there[s, :, lanes_of(halo[side])], whalo2[side, s])
+                mine[s, side] = (
+                    dot(there[s, :, lanes_of(edges[side])], whalo[side, s]) + jnp.where(n > SWITCH, old, 0.0)
+                )
+        if not finish:
+            force_into([(moved[s, g], slope_of(s, g), s, g) for s in range(segs) for g in inner], there)
+            beside(n + 1, 1 - slot)
+        for side in range(2):
+            arrival(n - 1, side).wait()
+        force_into(
+            [
+                (mine[s, side] + came[n - 1, side, s].astype(jnp.float32), slope_beyond(s, side), s, halo[side])
+                for s in range(segs)
+                for side in range(2)
+            ],
+            here,
+        )
+        for side in range(2):
+            g = edges[side]
+            for s in range(segs):
+                moved[s, g] = hold[slot, s, side] + dot(
+                    here[s, :, lanes_of((-1, pairs - 1)[side], 2)], w_edge[s, side, side * pair:(side + 2) * pair, :]
+                )
         if finish:
             for s in range(segs):
                 for g in range(pairs):
@@ -380,18 +429,38 @@
         else:
             force_into([(moved[s, g], slope_of(s, g), s, g) for s in range(segs) for g in edges], there)
 
-    step(0, 0, False, False)
+    count = (SWITCH - 1) // segs
+    size = pair // count
+    borders = [
+        [
+            pltpu.make_async_remote_copy(
+                src_ref=w_edge.at[s, side, pair + k * size:pair + (k + 1) * size, :],
+                dst_ref=whalo2.at[1 - side, s, k * size:(k + 1) * size, :],
+                send_sem=border_send.at[s * count + k, side], recv_sem=border_recv.at[s * count + k, side],
+                device_id={"blk": (left, right)[side]}, device_id_type=MESH,
+            )
+            for side in range(2)
+        ]
+        for s in range(segs)
+        for k in range(count)
+    ]
+    for n in range(SWITCH):
+        step(n, n % 2, n > 0, borders[n] if n < len(borders) else [])
     follow_copy.start()
     for x in gram_copies1:
         x.start()
-
-    def two(i, unused):
-        step(2 * i + 1, 1, True, False)
-        step(2 * i + 2, 0, True, False)
+    beside(SWITCH, 1)
+    for both in borders:
+        for x in both:
+            x.wait()
+
+    def two_late(i, unused):
+        late_step(SWITCH + 2 * i, 1, False)
+        late_step(SWITCH + 2 * i + 1, 0, False)
         return unused
 
-    lax.fori_loop(0, (STEPS - 2) // 2, two, 0)
-    step(STEPS - 1, 1, True, True)
+    lax.fori_loop(0, (STEPS - 1 - SWITCH) // 2, two_late, 0)
+    late_step(STEPS - 1, 1, True)
 
     gram2[me_seg] = total_of(gram1, gram_copies1, n_blk)
     gram_copies2 = everyone(gram2, me_seg, "seg", n_seg, gram_sem2)
@@ -420,6 +489,8 @@
     copies = everyone(part1, me_blk, "blk", n_blk, red_sem1)
     for x in copies:
         x.start()
+    for side in range(2):
+        arrival(STEPS - 1, side).wait()
     part2[me_seg] = total_of(part1, copies, n_blk)
     copies = everyone(part2, me_seg, "seg", n_seg, red_sem2)
     for x in copies:
@@ -511,7 +582,7 @@
             pltpu.SemaphoreType.DMA((segs, 2)),
             pltpu.SemaphoreType.DMA((4,)),
         ],
-        compiler_params=pltpu.CompilerParams(vmem_limit_bytes=48 << 20),
+        compiler_params=pltpu.CompilerParams(vmem_limit_bytes=56 << 20),
         cost_estimate=pl.CostEstimate(flops=8 * work, bytes_accessed=work, transcendentals=0),
         name="edge",
     )(base_flat, dir_flat, coupling, columns, wet, tiles)
@@ -546,14 +617,18 @@
             pltpu.VMEM((PAD, 2 * PAD), jnp.float32),
             pltpu.VMEM((tracers * rows, points), jnp.float32),
             pltpu.VMEM((2, segs, pair, pair), jnp.bfloat16),
-            pltpu.VMEM((STEPS - 1, 2, segs, PAD, pair), jnp.bfloat16),
-            pltpu.VMEM((STEPS - 1, 2, segs, PAD, pair), jnp.bfloat16),
+            pltpu.VMEM((2, segs, pair, pair), jnp.bfloat16),
+            pltpu.VMEM((2, segs, 2, PAD, pair), jnp.float32),
+            pltpu.VMEM((STEPS, 2, segs, PAD, pair), jnp.bfloat16),
+            pltpu.VMEM((STEPS, 2, segs, PAD, pair), jnp.bfloat16),
             pltpu.VMEM((n_blk, 16, points), jnp.float32),
             pltpu.VMEM((n_seg, 16, points), jnp.float32),
             pltpu.VMEM((n_blk, half, points), jnp.float32),
             pltpu.VMEM((n_seg, half, points), jnp.float32),
-            pltpu.SemaphoreType.DMA((STEPS - 1, 2)),
-            pltpu.SemaphoreType.DMA((STEPS - 1, 2)),
+            pltpu.SemaphoreType.DMA((STEPS, 2)),
+            pltpu.SemaphoreType.DMA((STEPS, 2)),
+            pltpu.SemaphoreType.DMA((SWITCH - 1, 2)),
+            pltpu.SemaphoreType.DMA((SWITCH - 1, 2)),
             pltpu.SemaphoreType.DMA((2,)),
             pltpu.SemaphoreType.DMA((2, n_blk - 1)),
             pltpu.SemaphoreType.DMA((2, n_seg - 1)),

time: 63.3 us -> 57.3 us (0.905)
  local copies, waits for them, and re-layouts: 5.11 us -> 1.22 us
  Pallas kernels: 50.6 us -> 48.5 us
    unnamed x20 -> x18, local copies, waits for them, and re-layouts: 5.11 us -> 1.22 us
    pallas_call x1, Pallas kernels: 42.6 us -> 39.6 us  [on_device(): pl.pallas_call(functools.partial(steps_kernel, dims), out_shape=(jax.Shap...]
    pallas_call x1, Pallas kernels: 4.74 us -> 5.47 us  [on_device(): pl.pallas_call(functools.partial(edge_kernel, dims), out_shape=(shape((se...]
  transfers between devices with their start and end apart: 2 -> 2, of which waited for: 2 -> 2; matrix products, arithmetic and copies ran while one was open for 0% -> 0% of each run, Pallas kernels for 5% -> 6%
where the time goes in v3:
time: 57.3 us; the launch traced here: 57.2 us
  Pallas kernels  48.5 us (85%)
  waiting for transfers between devices  4.19 us (7%)
  starting transfers between devices  2.52 us (4%)
  local copies, waits for them, and re-layouts  1.22 us (2%)
  between operations  0.73 us (1%)
    pallas_call x1, Pallas kernels, on_device(): pl.pallas_call(functools.partial(steps_kernel, dims), out_shape=(jax.Shap...  39.6 us
    pallas_call x1, Pallas kernels, on_device(): pl.pallas_call(functools.partial(edge_kernel, dims), out_shape=(shape((se...  5.47 us
    pallas_call x1, Pallas kernels, on_device(): pl.pallas_call(functools.partial(inner_kernel, dims), out_shape=(shape((s...  3.38 us
    ppermute x1, waiting for transfers between devices, on_device(): lax.ppermute(to_left, 'blk', [(i, (i + n_blk - 1) % n_blk) for i in ring])  2.59 us
    ppermute x1, starting transfers between devices, on_device(): lax.ppermute(to_left, 'blk', [(i, (i + n_blk - 1) % n_blk) for i in ring])  2.02 us
    ppermute x1, waiting for transfers between devices, on_device(): lax.ppermute(to_right, 'blk', [(i, (i + 1) % n_blk) for i in ring])  1.6 us
    unnamed x18, local copies, waits for them, and re-layouts  1.22 us
  transfers between devices with their start and end apart: 2, of which 2 were waited for; matrix products, arithmetic and copies ran while one was open for 0% of the time, Pallas kernels for 6%

profile of v3, /device:TPU:0, one launch (start us, length us, event | category | flops | bytes accessed | tf_op | source)
XLA Modules:
  0.0 57.2 jit_solution(1514748790380641235)
XLA Ops:
  0.6 0.0 copy-start
  0.6 0.0 copy-start.6
  0.7 0.0 copy-start.7
  0.7 5.5 %edge.1 = (bf16[2,2,768,256]{3,2,1,0:T(8,128)(2,1)}, f32[2,32,1024]{2,1,0:T(8,128)}, bf16[2,32,1024]{2,1,0:T(8,128)(2,1)}, bf16[2,576,128]{2,1,0:T(8,128)(2,1)}, bf16[2,576,128]{2,1,0:T(8,128)(2,1)}) custom-call(f32[320,128]{1,0:T(8,128)} %bitcast.9, f32[320,128]{1,0:T(8,128)} %bitcast.6, f32[20,20]{1,0:T(8,128)} %coup_ref.1, s32[2,8,16]{2,1,0:T(8,128)} %cols_ref.3, ...), custom_call_target="tpu_custom_call" | custom-call | flops 33554432 | bytes 4194304 | tf_op jit(solution)/shard_map/edge/pallas_call | solution.py:563
  6.1 0.5 collective-permute-start
  6.6 2.0 %collective-permute-start.1 = (bf16[2,576,128]{2,1,0:T(8,128)(2,1)}, bf16[2,576,128]{2,1,0:T(8,128)(2,1)S(1)}, u32[]{:S(2)}, u32[]{:S(2)}) collective-permute-start(bf16[2,576,128]{2,1,0:T(8,128)(2,1)} %get-tuple-element.16), channel_id=1, source_target_pairs={{0,3},{1,0},{2,1},{3,2},{4,7},{5,4},{6,5},{7,6},{8,11},{9,8},{10,9... | collective-permute-start | bytes 884744 | tf_op jit(solution)/shard_map/ppermute | solution.py:590
  8.7 0.0 copy-done
  8.7 0.0 copy-done.6
  8.7 0.0 copy-done.7
  8.7 0.0 copy-start.2
  8.7 0.0 copy-start.3
  8.7 0.0 copy-start.4
  8.7 0.0 copy-start.5
  8.7 3.4 %inner.1 = (bf16[2,2,768,256]{3,2,1,0:T(8,128)(2,1)S(1)}, f32[40,128]{1,0:T(8,128)S(1)}) custom-call(f32[8,320,128]{2,1,0:T(8,128)S(1)} %bitcast.4, s32[2,8,16]{2,1,0:T(8,128)S(1)} %copy-done.6, s32[8,128]{1,0:T(8,128)S(1)} %copy-done.7, bf16[2,8,16,128,128]{4,3,2,1,0:T(8,128)(2,1)} %tiles_ref.3), custom_call_target="tpu_custom_call" | custom-call | flops 33554432 | bytes 4194304 | tf_op jit(solution)/shard_map/inner/pallas_call | solution.py:592
  12.1 1.6 %collective-permute-done.from_left = bf16[2,576,128]{2,1,0:T(8,128)(2,1)S(1)} collective-permute-done((bf16[2,576,128]{2,1,0:T(8,128)(2,1)}, bf16[2,576,128]{2,1,0:T(8,128)(2,1)S(1)}, u32[]{:S(2)}, u32[]{:S(2)}) %collective-permute-start) | collective-permute-done | bytes 294944 | tf_op jit(solution)/shard_map/ppermute | solution.py:591
  13.7 2.6 %collective-permute-done.1.from_right = bf16[2,576,128]{2,1,0:T(8,128)(2,1)S(1)} collective-permute-done((bf16[2,576,128]{2,1,0:T(8,128)(2,1)}, bf16[2,576,128]{2,1,0:T(8,128)(2,1)S(1)}, u32[]{:S(2)}, u32[]{:S(2)}) %collective-permute-start.1) | collective-permute-done | bytes 294944 | tf_op jit(solution)/shard_map/ppermute | solution.py:590
  16.3 0.0 copy-done.1
  16.3 0.0 copy-done.2
  16.3 0.0 copy-done.3
  16.3 0.0 copy-done.4
  16.3 0.0 copy-done.5
  16.3 39.6 %steps.1 = (f32[320,128]{1,0:T(8,128)S(1)}, f32[9]{0:T(128)S(1)}) custom-call(f32[2,32,1024]{2,1,0:T(8,128)S(1)} %copy-done.3, bf16[2,32,1024]{2,1,0:T(8,128)(2,1)S(1)} %copy-done.4, f32[320,128]{1,0:T(8,128)S(1)} %bitcast.7, f32[20,20]{1,0:T(8,128)S(1)} %copy-done.5, bf16[2,2,768,256]{3,2,1,0:T(8,128)(2,1)S(1)} %copy-done.1, ...), custom_call_target="tpu_custom_call" | custom-call | tf_op jit(solution)/shard_map/steps/pallas_call | solution.py:606
  56.0 0.7 %copy.11 = f32[2,20,8,128]{3,2,1,0:T(8,128)} copy(f32[2,20,8,128]{3,2,1,0:T(8,128)S(1)} %bitcast.8) | data formatting | bytes 327680
  56.6 0.5 copy.12
  (1 shorter events, 0.0 us)
Async XLA Ops:
  0.6 8.0 %copy-start = (f32[8,2,20,8,128]{4,3,2,1,0:T(8,128)S(1)}, f32[8,2,20,8,128]{4,3,2,1,0:T(8,128)}, u32[]{:S(2)}) copy-start(f32[8,2,20,8,128]{4,3,2,1,0:T(8,128)} %param.13) | copy-start | bytes 3932164
  0.6 8.0 %copy-start.6 = (s32[2,8,16]{2,1,0:T(8,128)S(1)}, s32[2,8,16]{2,1,0:T(8,128)}, u32[]{:S(2)}) copy-start(s32[2,8,16]{2,1,0:T(8,128)} %cols_ref.3) | copy-start | bytes 3076
  0.7 8.0 %copy-start.7 = (s32[8,128]{1,0:T(8,128)S(1)}, s32[8,128]{1,0:T(8,128)}, u32[]{:S(2)}) copy-start(s32[8,128]{1,0:T(8,128)} %wet_ref.3) | copy-start | bytes 12292
  6.1 7.6 %collective-permute-start = (bf16[2,576,128]{2,1,0:T(8,128)(2,1)}, bf16[2,576,128]{2,1,0:T(8,128)(2,1)S(1)}, u32[]{:S(2)}, u32[]{:S(2)}) collective-permute-start(bf16[2,576,128]{2,1,0:T(8,128)(2,1)} %get-tuple-element.15), channel_id=1, source_target_pairs={{0,1},{1,2},{2,3},{3,0},{4,5},{5,6},{6,7},{7,4},{8,9},{9,10},{10,1... | collective-permute-start | bytes 884744 | tf_op jit(solution)/shard_map/ppermute | solution.py:591
  6.6 9.7 %collective-permute-start.1 = (bf16[2,576,128]{2,1,0:T(8,128)(2,1)}, bf16[2,576,128]{2,1,0:T(8,128)(2,1)S(1)}, u32[]{:S(2)}, u32[]{:S(2)}) collective-permute-start(bf16[2,576,128]{2,1,0:T(8,128)(2,1)} %get-tuple-element.16), channel_id=1, source_target_pairs={{0,3},{1,0},{2,1},{3,2},{4,7},{5,4},{6,5},{7,6},{8,11},{9,8},{10,9... | collective-permute-start | bytes 884744 | tf_op jit(solution)/shard_map/ppermute | solution.py:590
  8.7 7.6 %copy-start.1 = (bf16[2,2,768,256]{3,2,1,0:T(8,128)(2,1)S(1)}, bf16[2,2,768,256]{3,2,1,0:T(8,128)(2,1)}, u32[]{:S(2)}) copy-start(bf16[2,2,768,256]{3,2,1,0:T(8,128)(2,1)} %get-tuple-element.13.w_edge) | copy-start | bytes 4718596
  8.7 7.6 %copy-start.2 = (f32[2,20,8,128]{3,2,1,0:T(8,128)S(1)}, f32[2,20,8,128]{3,2,1,0:T(8,128)}, u32[]{:S(2)}) copy-start(f32[2,20,8,128]{3,2,1,0:T(8,128)} %param.8) | copy-start | bytes 491524
  8.7 7.6 %copy-start.3 = (f32[2,32,1024]{2,1,0:T(8,128)S(1)}, f32[2,32,1024]{2,1,0:T(8,128)}, u32[]{:S(2)}) copy-start(f32[2,32,1024]{2,1,0:T(8,128)} %get-tuple-element.11.slope) | copy-start | bytes 786436
  8.7 7.6 %copy-start.4 = (bf16[2,32,1024]{2,1,0:T(8,128)(2,1)S(1)}, bf16[2,32,1024]{2,1,0:T(8,128)(2,1)}, u32[]{:S(2)}) copy-start(bf16[2,32,1024]{2,1,0:T(8,128)(2,1)} %get-tuple-element.12.start) | copy-start | bytes 393220
  8.7 7.6 %copy-start.5 = (f32[20,20]{1,0:T(8,128)S(1)}, f32[20,20]{1,0:T(8,128)}, u32[]{:S(2)}) copy-start(f32[20,20]{1,0:T(8,128)} %coup_ref.1) | copy-start | bytes 4804

commit v4 on v3

--- a/solution.py
+++ b/solution.py
@@ -167,8 +167,7 @@
         drive_v[s, :, g * pair:(g + 1) * pair] = d
         if g in edges:
             high = k.astype(jnp.bfloat16)
-            low = (k - high.astype(jnp.float32)).astype(jnp.bfloat16)
-            for i, x in enumerate((d, high, low)):
+            for i, x in enumerate((d, high)):
                 for j in range(2):
                     at = 3 * points + (2 * i + j) * PAD
                     out_v[edges.index(g), s, at:at + PAD, :] = x[:, j * points:(j + 1) * points]
@@ -227,7 +226,7 @@
 
 def steps_kernel(
     dims, slope, start, dir_ref, coup_ref, w_edge, w_inner, from_left, from_right, gram_in, basis, orth_ref, coef_ref,
-    drive0, drive1, cc, follow, whalo, whalo2, hold, sent, came, part1, part2, gram1, gram2,
+    drive0, drive1, cc, follow, shalo, whalo, whalo2, hold, sent, came, part1, part2, gram1, gram2,
     send_sem, recv_sem, border_send, border_recv, follow_sem, red_sem1, red_sem2, gram_sem1, gram_sem2,
 ):
     segs, tracers, rows, points, kry, n_seg, n_blk, entries = dims
@@ -264,7 +263,7 @@
         return jnp.concatenate([ref[s, at:at + PAD, :], ref[s, at + PAD:at + 2 * PAD, :]], axis=1)
 
     def slope_beyond(s, side):
-        return beyond(s, side, 1).astype(jnp.float32) + beyond(s, side, 2).astype(jnp.float32)
+        return shalo[side, s]
 
     edges = (0, pairs - 1)
     inner = range(1, pairs - 1)
@@ -273,6 +272,7 @@
         drive0[s, :, pair:(pairs + 1) * pair] = start[s]
         for side in range(2):
             drive0[s, :, lanes_of(halo[side])] = beyond(s, side, 0)
+            shalo[side, s] = beyond(s, side, 1).astype(jnp.float32)
             whalo[side, s] = jnp.zeros((pair, pair), jnp.bfloat16)
             for n, (c, j) in enumerate(BORDER[1 - side]):
                 whalo[side, s, c * points:(c + 1) * points, j * points:(j + 1) * points] = (
@@ -559,7 +559,7 @@
 
     dims = (segs, tracers, rows, points, total)
     work = segs * rows * stored * points * points
-    border = shape((segs, 3 * points + 6 * PAD, points), bf16)
+    border = shape((segs, 3 * points + 4 * PAD, points), bf16)
     w_edge, slope, start, to_left, to_right = pl.pallas_call(
         functools.partial(edge_kernel, dims),
         out_shape=(
@@ -576,7 +576,7 @@
             pltpu.VMEM((segs, 2, wide * points, pair), bf16),
             pltpu.VMEM((segs, PAD, rows * points), f32),
             pltpu.VMEM((segs, PAD, rows * points), bf16),
-            pltpu.VMEM((2, segs, 3 * points + 6 * PAD, points), bf16),
+            pltpu.VMEM((2, segs, 3 * points + 4 * PAD, points), bf16),
         ] + sems_of(2) + [
             pltpu.SemaphoreType.DMA((3,)),
             pltpu.SemaphoreType.DMA((segs, 2)),
@@ -616,6 +616,7 @@
             pltpu.VMEM((segs, PAD, (pairs + 2) * pair), jnp.bfloat16),
             pltpu.VMEM((PAD, 2 * PAD), jnp.float32),
             pltpu.VMEM((tracers * rows, points), jnp.float32),
+            pltpu.VMEM((2, segs, PAD, pair), jnp.float32),
             pltpu.VMEM((2, segs, pair, pair), jnp.bfloat16),
             pltpu.VMEM((2, segs, pair, pair), jnp.bfloat16),
             pltpu.VMEM((2, segs, 2, PAD, pair), jnp.float32),

time: 57.3 us -> 56.5 us (0.986)
  waiting for transfers between devices: 4.19 us -> 3.49 us
    ppermute x1, waiting for transfers between devices: 1.6 us -> 0.9 us  [on_device(): lax.ppermute(to_right, 'blk', [(i, (i + 1) % n_blk) for i in ring])]
where the time goes in v4:
time: 56.5 us; the launch traced here: 56.3 us
  Pallas kernels  48.4 us (86%)
  waiting for transfers between devices  3.49 us (6%)
  starting transfers between devices  2.52 us (4%)
  local copies, waits for them, and re-layouts  1.22 us (2%)
  between operations  0.73 us (1%)
    pallas_call x1, Pallas kernels, on_device(): pl.pallas_call(functools.partial(steps_kernel, dims), out_shape=(jax.Shap...  39.6 us
    pallas_call x1, Pallas kernels, on_device(): pl.pallas_call(functools.partial(edge_kernel, dims), out_shape=(shape((se...  5.39 us
    pallas_call x1, Pallas kernels, on_device(): pl.pallas_call(functools.partial(inner_kernel, dims), out_shape=(shape((s...  3.38 us
    ppermute x1, waiting for transfers between devices, on_device(): lax.ppermute(to_left, 'blk', [(i, (i + n_blk - 1) % n_blk) for i in ring])  2.59 us
    ppermute x1, starting transfers between devices, on_device(): lax.ppermute(to_left, 'blk', [(i, (i + n_blk - 1) % n_blk) for i in ring])  2.01 us
    unnamed x18, local copies, waits for them, and re-layouts  1.22 us
  transfers between devices with their start and end apart: 2, of which 2 were waited for; matrix products, arithmetic and copies ran while one was open for 0% of the time, Pallas kernels for 6%

profile of v4, /device:TPU:0, one launch (start us, length us, event | category | flops | bytes accessed | tf_op | source)
XLA Modules:
  0.0 56.3 jit_solution(9978470241567352105)
XLA Ops:
  0.6 0.0 copy-start
  0.6 0.0 copy-start.6
  0.7 0.0 copy-start.7
  0.7 5.4 %edge.1 = (bf16[2,2,768,256]{3,2,1,0:T(8,128)(2,1)}, f32[2,32,1024]{2,1,0:T(8,128)}, bf16[2,32,1024]{2,1,0:T(8,128)(2,1)}, bf16[2,512,128]{2,1,0:T(8,128)(2,1)}, bf16[2,512,128]{2,1,0:T(8,128)(2,1)}) custom-call(f32[320,128]{1,0:T(8,128)} %bitcast.9, f32[320,128]{1,0:T(8,128)} %bitcast.6, f32[20,20]{1,0:T(8,128)} %coup_ref.1, s32[2,8,16]{2,1,0:T(8,128)} %cols_ref.3, ...), custom_call_target="tpu_custom_call" | custom-call | flops 33554432 | bytes 4194304 | tf_op jit(solution)/shard_map/edge/pallas_call | solution.py:563
  6.1 0.5 collective-permute-start
  6.6 2.0 %collective-permute-start.1 = (bf16[2,512,128]{2,1,0:T(8,128)(2,1)}, bf16[2,512,128]{2,1,0:T(8,128)(2,1)S(1)}, u32[]{:S(2)}, u32[]{:S(2)}) collective-permute-start(bf16[2,512,128]{2,1,0:T(8,128)(2,1)} %get-tuple-element.16), channel_id=1, source_target_pairs={{0,3},{1,0},{2,1},{3,2},{4,7},{5,4},{6,5},{7,6},{8,11},{9,8},{10,9... | collective-permute-start | bytes 786440 | tf_op jit(solution)/shard_map/ppermute | solution.py:590
  8.6 0.0 copy-done
  8.6 0.0 copy-done.6
  8.6 0.0 copy-done.7
  8.6 0.0 copy-start.2
  8.6 0.0 copy-start.3
  8.6 0.0 copy-start.4
  8.6 0.0 copy-start.5
  8.6 3.4 %inner.1 = (bf16[2,2,768,256]{3,2,1,0:T(8,128)(2,1)S(1)}, f32[40,128]{1,0:T(8,128)S(1)}) custom-call(f32[8,320,128]{2,1,0:T(8,128)S(1)} %bitcast.4, s32[2,8,16]{2,1,0:T(8,128)S(1)} %copy-done.6, s32[8,128]{1,0:T(8,128)S(1)} %copy-done.7, bf16[2,8,16,128,128]{4,3,2,1,0:T(8,128)(2,1)} %tiles_ref.3), custom_call_target="tpu_custom_call" | custom-call | flops 33554432 | bytes 4194304 | tf_op jit(solution)/shard_map/inner/pallas_call | solution.py:592
  12.0 0.9 %collective-permute-done.from_left = bf16[2,512,128]{2,1,0:T(8,128)(2,1)S(1)} collective-permute-done((bf16[2,512,128]{2,1,0:T(8,128)(2,1)}, bf16[2,512,128]{2,1,0:T(8,128)(2,1)S(1)}, u32[]{:S(2)}, u32[]{:S(2)}) %collective-permute-start) | collective-permute-done | bytes 262176 | tf_op jit(solution)/shard_map/ppermute | solution.py:591
  12.9 2.6 %collective-permute-done.1.from_right = bf16[2,512,128]{2,1,0:T(8,128)(2,1)S(1)} collective-permute-done((bf16[2,512,128]{2,1,0:T(8,128)(2,1)}, bf16[2,512,128]{2,1,0:T(8,128)(2,1)S(1)}, u32[]{:S(2)}, u32[]{:S(2)}) %collective-permute-start.1) | collective-permute-done | bytes 262176 | tf_op jit(solution)/shard_map/ppermute | solution.py:590
  15.5 0.0 copy-done.1
  15.5 0.0 copy-done.2
  15.5 0.0 copy-done.3
  15.5 0.0 copy-done.4
  15.5 0.0 copy-done.5
  15.5 39.6 %steps.1 = (f32[320,128]{1,0:T(8,128)S(1)}, f32[9]{0:T(128)S(1)}) custom-call(f32[2,32,1024]{2,1,0:T(8,128)S(1)} %copy-done.3, bf16[2,32,1024]{2,1,0:T(8,128)(2,1)S(1)} %copy-done.4, f32[320,128]{1,0:T(8,128)S(1)} %bitcast.7, f32[20,20]{1,0:T(8,128)S(1)} %copy-done.5, bf16[2,2,768,256]{3,2,1,0:T(8,128)(2,1)S(1)} %copy-done.1, ...), custom_call_target="tpu_custom_call" | custom-call | tf_op jit(solution)/shard_map/steps/pallas_call | solution.py:606
  55.2 0.7 %copy.11 = f32[2,20,8,128]{3,2,1,0:T(8,128)} copy(f32[2,20,8,128]{3,2,1,0:T(8,128)S(1)} %bitcast.8) | data formatting | bytes 327680
  55.8 0.5 copy.12
  (1 shorter events, 0.0 us)
Async XLA Ops:
  0.6 8.0 %copy-start = (f32[8,2,20,8,128]{4,3,2,1,0:T(8,128)S(1)}, f32[8,2,20,8,128]{4,3,2,1,0:T(8,128)}, u32[]{:S(2)}) copy-start(f32[8,2,20,8,128]{4,3,2,1,0:T(8,128)} %param.13) | copy-start | bytes 3932164
  0.6 7.9 %copy-start.6 = (s32[2,8,16]{2,1,0:T(8,128)S(1)}, s32[2,8,16]{2,1,0:T(8,128)}, u32[]{:S(2)}) copy-start(s32[2,8,16]{2,1,0:T(8,128)} %cols_ref.3) | copy-start | bytes 3076
  0.7 7.9 %copy-start.7 = (s32[8,128]{1,0:T(8,128)S(1)}, s32[8,128]{1,0:T(8,128)}, u32[]{:S(2)}) copy-start(s32[8,128]{1,0:T(8,128)} %wet_ref.3) | copy-start | bytes 12292
  6.1 6.9 %collective-permute-start = (bf16[2,512,128]{2,1,0:T(8,128)(2,1)}, bf16[2,512,128]{2,1,0:T(8,128)(2,1)S(1)}, u32[]{:S(2)}, u32[]{:S(2)}) collective-permute-start(bf16[2,512,128]{2,1,0:T(8,128)(2,1)} %get-tuple-element.15), channel_id=1, source_target_pairs={{0,1},{1,2},{2,3},{3,0},{4,5},{5,6},{6,7},{7,4},{8,9},{9,10},{10,1... | collective-permute-start | bytes 786440 | tf_op jit(solution)/shard_map/ppermute | solution.py:591
  6.6 9.0 %collective-permute-start.1 = (bf16[2,512,128]{2,1,0:T(8,128)(2,1)}, bf16[2,512,128]{2,1,0:T(8,128)(2,1)S(1)}, u32[]{:S(2)}, u32[]{:S(2)}) collective-permute-start(bf16[2,512,128]{2,1,0:T(8,128)(2,1)} %get-tuple-element.16), channel_id=1, source_target_pairs={{0,3},{1,0},{2,1},{3,2},{4,7},{5,4},{6,5},{7,6},{8,11},{9,8},{10,9... | collective-permute-start | bytes 786440 | tf_op jit(solution)/shard_map/ppermute | solution.py:590
  8.6 6.9 %copy-start.1 = (bf16[2,2,768,256]{3,2,1,0:T(8,128)(2,1)S(1)}, bf16[2,2,768,256]{3,2,1,0:T(8,128)(2,1)}, u32[]{:S(2)}) copy-start(bf16[2,2,768,256]{3,2,1,0:T(8,128)(2,1)} %get-tuple-element.13.w_edge) | copy-start | bytes 4718596
  8.6 6.9 %copy-start.2 = (f32[2,20,8,128]{3,2,1,0:T(8,128)S(1)}, f32[2,20,8,128]{3,2,1,0:T(8,128)}, u32[]{:S(2)}) copy-start(f32[2,20,8,128]{3,2,1,0:T(8,128)} %param.8) | copy-start | bytes 491524
  8.6 6.9 %copy-start.3 = (f32[2,32,1024]{2,1,0:T(8,128)S(1)}, f32[2,32,1024]{2,1,0:T(8,128)}, u32[]{:S(2)}) copy-start(f32[2,32,1024]{2,1,0:T(8,128)} %get-tuple-element.11.slope) | copy-start | bytes 786436
  8.6 6.9 %copy-start.4 = (bf16[2,32,1024]{2,1,0:T(8,128)(2,1)S(1)}, bf16[2,32,1024]{2,1,0:T(8,128)(2,1)}, u32[]{:S(2)}) copy-start(bf16[2,32,1024]{2,1,0:T(8,128)(2,1)} %get-tuple-element.12.start) | copy-start | bytes 393220
  8.6 6.9 %copy-start.5 = (f32[20,20]{1,0:T(8,128)S(1)}, f32[20,20]{1,0:T(8,128)}, u32[]{:S(2)}) copy-start(f32[20,20]{1,0:T(8,128)} %coup_ref.1) | copy-start | bytes 4804

commit v5 on v4

--- a/solution.py
+++ b/solution.py
@@ -28,14 +28,14 @@
             accs[j][d] += tile_at(j, k).astype(jnp.float32)
         return unused
 
-    lax.fori_loop(0, stored, add, 0, unroll=4)
+    lax.fori_loop(0, stored, add, 0, unroll=8)
     size = accs[0].shape[1]
     for j in range(2):
-        mask = wet(row + j).astype(jnp.float32)
+        mask = wet(row + j).astype(jnp.float32).astype(jnp.bfloat16)
         for c in range(wide + 1):
             d = c - j
             if 0 <= d < wide:
-                put(c, j, (accs[j][d].T * mask).astype(jnp.bfloat16))
+                put(c, j, accs[j][d].astype(jnp.bfloat16).T * mask)
             else:
                 put(c, j, jnp.zeros((size, size), jnp.bfloat16))
 

time: 56.5 us -> 56 us (level)
  Pallas kernels: 48.4 us -> 47.4 us
  transfers between devices with their start and end apart: 2 -> 2, of which waited for: 2 -> 2; matrix products, arithmetic and copies ran while one was open for 0% -> 0% of each run, Pallas kernels for 6% -> 5%
where the time goes in v5:
time: 56 us; the launch traced here: 55.9 us
  Pallas kernels  47.4 us (85%)
  waiting for transfers between devices  3.96 us (7%)
  starting transfers between devices  2.52 us (4%)
  local copies, waits for them, and re-layouts  1.22 us (2%)
  between operations  0.73 us (1%)
    pallas_call x1, Pallas kernels, on_device(): pl.pallas_call(functools.partial(steps_kernel, dims), out_shape=(jax.Shap...  39.6 us
    pallas_call x1, Pallas kernels, on_device(): pl.pallas_call(functools.partial(edge_kernel, dims), out_shape=(shape((se...  4.9 us
    pallas_call x1, Pallas kernels, on_device(): pl.pallas_call(functools.partial(inner_kernel, dims), out_shape=(shape((s...  2.91 us
    ppermute x1, waiting for transfers between devices, on_device(): lax.ppermute(to_left, 'blk', [(i, (i + n_blk - 1) % n_blk) for i in ring])  2.59 us
    ppermute x1, starting transfers between devices, on_device(): lax.ppermute(to_left, 'blk', [(i, (i + n_blk - 1) % n_blk) for i in ring])  2.01 us
    ppermute x1, waiting for transfers between devices, on_device(): lax.ppermute(to_right, 'blk', [(i, (i + 1) % n_blk) for i in ring])  1.36 us
    unnamed x18, local copies, waits for them, and re-layouts  1.22 us
  transfers between devices with their start and end apart: 2, of which 2 were waited for; matrix products, arithmetic and copies ran while one was open for 0% of the time, Pallas kernels for 5%

profile of v5, /device:TPU:0, one launch (start us, length us, event | category | flops | bytes accessed | tf_op | source)
XLA Modules:
  0.0 55.9 jit_solution(6246045199781456795)
XLA Ops:
  0.6 0.0 copy-start
  0.6 0.0 copy-start.6
  0.7 0.0 copy-start.7
  0.7 4.9 %edge.1 = (bf16[2,2,768,256]{3,2,1,0:T(8,128)(2,1)}, f32[2,32,1024]{2,1,0:T(8,128)}, bf16[2,32,1024]{2,1,0:T(8,128)(2,1)}, bf16[2,512,128]{2,1,0:T(8,128)(2,1)}, bf16[2,512,128]{2,1,0:T(8,128)(2,1)}) custom-call(f32[320,128]{1,0:T(8,128)} %bitcast.9, f32[320,128]{1,0:T(8,128)} %bitcast.6, f32[20,20]{1,0:T(8,128)} %coup_ref.1, s32[2,8,16]{2,1,0:T(8,128)} %cols_ref.3, ...), custom_call_target="tpu_custom_call" | custom-call | flops 33554432 | bytes 4194304 | tf_op jit(solution)/shard_map/edge/pallas_call | solution.py:563
  5.6 0.5 collective-permute-start
  6.1 2.0 %collective-permute-start.1 = (bf16[2,512,128]{2,1,0:T(8,128)(2,1)}, bf16[2,512,128]{2,1,0:T(8,128)(2,1)S(1)}, u32[]{:S(2)}, u32[]{:S(2)}) collective-permute-start(bf16[2,512,128]{2,1,0:T(8,128)(2,1)} %get-tuple-element.16), channel_id=1, source_target_pairs={{0,3},{1,0},{2,1},{3,2},{4,7},{5,4},{6,5},{7,6},{8,11},{9,8},{10,9... | collective-permute-start | bytes 786440 | tf_op jit(solution)/shard_map/ppermute | solution.py:590
  8.1 0.0 copy-done
  8.1 0.0 copy-done.6
  8.1 0.0 copy-done.7
  8.1 0.0 copy-start.2
  8.1 0.0 copy-start.3
  8.1 0.0 copy-start.4
  8.1 0.0 copy-start.5
  8.1 2.9 %inner.1 = (bf16[2,2,768,256]{3,2,1,0:T(8,128)(2,1)S(1)}, f32[40,128]{1,0:T(8,128)S(1)}) custom-call(f32[8,320,128]{2,1,0:T(8,128)S(1)} %bitcast.4, s32[2,8,16]{2,1,0:T(8,128)S(1)} %copy-done.6, s32[8,128]{1,0:T(8,128)S(1)} %copy-done.7, bf16[2,8,16,128,128]{4,3,2,1,0:T(8,128)(2,1)} %tiles_ref.3), custom_call_target="tpu_custom_call" | custom-call | flops 33554432 | bytes 4194304 | tf_op jit(solution)/shard_map/inner/pallas_call | solution.py:592
  11.1 1.4 %collective-permute-done.from_left = bf16[2,512,128]{2,1,0:T(8,128)(2,1)S(1)} collective-permute-done((bf16[2,512,128]{2,1,0:T(8,128)(2,1)}, bf16[2,512,128]{2,1,0:T(8,128)(2,1)S(1)}, u32[]{:S(2)}, u32[]{:S(2)}) %collective-permute-start) | collective-permute-done | bytes 262176 | tf_op jit(solution)/shard_map/ppermute | solution.py:591
  12.4 2.6 %collective-permute-done.1.from_right = bf16[2,512,128]{2,1,0:T(8,128)(2,1)S(1)} collective-permute-done((bf16[2,512,128]{2,1,0:T(8,128)(2,1)}, bf16[2,512,128]{2,1,0:T(8,128)(2,1)S(1)}, u32[]{:S(2)}, u32[]{:S(2)}) %collective-permute-start.1) | collective-permute-done | bytes 262176 | tf_op jit(solution)/shard_map/ppermute | solution.py:590
  15.0 0.0 copy-done.1
  15.0 0.0 copy-done.2
  15.0 0.0 copy-done.3
  15.0 0.0 copy-done.4
  15.0 0.0 copy-done.5
  15.1 39.6 %steps.1 = (f32[320,128]{1,0:T(8,128)S(1)}, f32[9]{0:T(128)S(1)}) custom-call(f32[2,32,1024]{2,1,0:T(8,128)S(1)} %copy-done.3, bf16[2,32,1024]{2,1,0:T(8,128)(2,1)S(1)} %copy-done.4, f32[320,128]{1,0:T(8,128)S(1)} %bitcast.7, f32[20,20]{1,0:T(8,128)S(1)} %copy-done.5, bf16[2,2,768,256]{3,2,1,0:T(8,128)(2,1)S(1)} %copy-done.1, ...), custom_call_target="tpu_custom_call" | custom-call | tf_op jit(solution)/shard_map/steps/pallas_call | solution.py:606
  54.7 0.7 %copy.11 = f32[2,20,8,128]{3,2,1,0:T(8,128)} copy(f32[2,20,8,128]{3,2,1,0:T(8,128)S(1)} %bitcast.8) | data formatting | bytes 327680
  55.3 0.5 copy.12
  (1 shorter events, 0.0 us)
Async XLA Ops:
  0.6 7.5 %copy-start = (f32[8,2,20,8,128]{4,3,2,1,0:T(8,128)S(1)}, f32[8,2,20,8,128]{4,3,2,1,0:T(8,128)}, u32[]{:S(2)}) copy-start(f32[8,2,20,8,128]{4,3,2,1,0:T(8,128)} %param.13) | copy-start | bytes 3932164
  0.6 7.5 %copy-start.6 = (s32[2,8,16]{2,1,0:T(8,128)S(1)}, s32[2,8,16]{2,1,0:T(8,128)}, u32[]{:S(2)}) copy-start(s32[2,8,16]{2,1,0:T(8,128)} %cols_ref.3) | copy-start | bytes 3076
  0.7 7.4 %copy-start.7 = (s32[8,128]{1,0:T(8,128)S(1)}, s32[8,128]{1,0:T(8,128)}, u32[]{:S(2)}) copy-start(s32[8,128]{1,0:T(8,128)} %wet_ref.3) | copy-start | bytes 12292
  5.6 6.9 %collective-permute-start = (bf16[2,512,128]{2,1,0:T(8,128)(2,1)}, bf16[2,512,128]{2,1,0:T(8,128)(2,1)S(1)}, u32[]{:S(2)}, u32[]{:S(2)}) collective-permute-start(bf16[2,512,128]{2,1,0:T(8,128)(2,1)} %get-tuple-element.15), channel_id=1, source_target_pairs={{0,1},{1,2},{2,3},{3,0},{4,5},{5,6},{6,7},{7,4},{8,9},{9,10},{10,1... | collective-permute-start | bytes 786440 | tf_op jit(solution)/shard_map/ppermute | solution.py:591
  6.1 9.0 %collective-permute-start.1 = (bf16[2,512,128]{2,1,0:T(8,128)(2,1)}, bf16[2,512,128]{2,1,0:T(8,128)(2,1)S(1)}, u32[]{:S(2)}, u32[]{:S(2)}) collective-permute-start(bf16[2,512,128]{2,1,0:T(8,128)(2,1)} %get-tuple-element.16), channel_id=1, source_target_pairs={{0,3},{1,0},{2,1},{3,2},{4,7},{5,4},{6,5},{7,6},{8,11},{9,8},{10,9... | collective-permute-start | bytes 786440 | tf_op jit(solution)/shard_map/ppermute | solution.py:590
  8.1 6.9 %copy-start.1 = (bf16[2,2,768,256]{3,2,1,0:T(8,128)(2,1)S(1)}, bf16[2,2,768,256]{3,2,1,0:T(8,128)(2,1)}, u32[]{:S(2)}) copy-start(bf16[2,2,768,256]{3,2,1,0:T(8,128)(2,1)} %get-tuple-element.13.w_edge) | copy-start | bytes 4718596
  8.1 6.9 %copy-start.2 = (f32[2,20,8,128]{3,2,1,0:T(8,128)S(1)}, f32[2,20,8,128]{3,2,1,0:T(8,128)}, u32[]{:S(2)}) copy-start(f32[2,20,8,128]{3,2,1,0:T(8,128)} %param.8) | copy-start | bytes 491524
  8.1 6.9 %copy-start.3 = (f32[2,32,1024]{2,1,0:T(8,128)S(1)}, f32[2,32,1024]{2,1,0:T(8,128)}, u32[]{:S(2)}) copy-start(f32[2,32,1024]{2,1,0:T(8,128)} %get-tuple-element.11.slope) | copy-start | bytes 786436
  8.1 6.9 %copy-start.4 = (bf16[2,32,1024]{2,1,0:T(8,128)(2,1)S(1)}, bf16[2,32,1024]{2,1,0:T(8,128)(2,1)}, u32[]{:S(2)}) copy-start(bf16[2,32,1024]{2,1,0:T(8,128)(2,1)} %get-tuple-element.12.start) | copy-start | bytes 393220
  8.1 6.9 %copy-start.5 = (f32[20,20]{1,0:T(8,128)S(1)}, f32[20,20]{1,0:T(8,128)}, u32[]{:S(2)}) copy-start(f32[20,20]{1,0:T(8,128)} %coup_ref.1) | copy-start | bytes 4804

commit v6 on v5

--- a/solution.py
+++ b/solution.py
@@ -518,7 +518,7 @@
         orth_ref[at, :] = orth_ref[at, :] - a
         return unused
 
-    lax.fori_loop(0, chunks, subtract, 0, unroll=4)
+    lax.fori_loop(0, chunks, subtract, 0, unroll=8)
 
 
 def hv_sum(terms):

time: 56 us -> 56 us (level)
  no operation moved by 1% of the time
where the time goes in v6:
time: 56 us; the launch traced here: 55.8 us
  Pallas kernels  47.4 us (85%)
  waiting for transfers between devices  3.96 us (7%)
  starting transfers between devices  2.52 us (4%)
  local copies, waits for them, and re-layouts  1.22 us (2%)
  between operations  0.73 us (1%)
    pallas_call x1, Pallas kernels, on_device(): pl.pallas_call(functools.partial(steps_kernel, dims), out_shape=(jax.Shap...  39.6 us
    pallas_call x1, Pallas kernels, on_device(): pl.pallas_call(functools.partial(edge_kernel, dims), out_shape=(shape((se...  4.9 us
    pallas_call x1, Pallas kernels, on_device(): pl.pallas_call(functools.partial(inner_kernel, dims), out_shape=(shape((s...  2.91 us
    ppermute x1, waiting for transfers between devices, on_device(): lax.ppermute(to_left, 'blk', [(i, (i + n_blk - 1) % n_blk) for i in ring])  2.59 us
    ppermute x1, starting transfers between devices, on_device(): lax.ppermute(to_left, 'blk', [(i, (i + n_blk - 1) % n_blk) for i in ring])  2.01 us
    ppermute x1, waiting for transfers between devices, on_device(): lax.ppermute(to_right, 'blk', [(i, (i + 1) % n_blk) for i in ring])  1.36 us
    unnamed x18, local copies, waits for them, and re-layouts  1.22 us
  transfers between devices with their start and end apart: 2, of which 2 were waited for; matrix products, arithmetic and copies ran while one was open for 0% of the time, Pallas kernels for 5%

profile of v6, /device:TPU:0, one launch (start us, length us, event | category | flops | bytes accessed | tf_op | source)
XLA Modules:
  0.0 55.8 jit_solution(17217147482895851472)
XLA Ops:
  0.6 0.0 copy-start
  0.6 0.0 copy-start.6
  0.7 0.0 copy-start.7
  0.7 4.9 %edge.1 = (bf16[2,2,768,256]{3,2,1,0:T(8,128)(2,1)}, f32[2,32,1024]{2,1,0:T(8,128)}, bf16[2,32,1024]{2,1,0:T(8,128)(2,1)}, bf16[2,512,128]{2,1,0:T(8,128)(2,1)}, bf16[2,512,128]{2,1,0:T(8,128)(2,1)}) custom-call(f32[320,128]{1,0:T(8,128)} %bitcast.9, f32[320,128]{1,0:T(8,128)} %bitcast.6, f32[20,20]{1,0:T(8,128)} %coup_ref.1, s32[2,8,16]{2,1,0:T(8,128)} %cols_ref.3, ...), custom_call_target="tpu_custom_call" | custom-call | flops 33554432 | bytes 4194304 | tf_op jit(solution)/shard_map/edge/pallas_call | solution.py:563
  5.6 0.5 collective-permute-start
  6.1 2.0 %collective-permute-start.1 = (bf16[2,512,128]{2,1,0:T(8,128)(2,1)}, bf16[2,512,128]{2,1,0:T(8,128)(2,1)S(1)}, u32[]{:S(2)}, u32[]{:S(2)}) collective-permute-start(bf16[2,512,128]{2,1,0:T(8,128)(2,1)} %get-tuple-element.16), channel_id=1, source_target_pairs={{0,3},{1,0},{2,1},{3,2},{4,7},{5,4},{6,5},{7,6},{8,11},{9,8},{10,9... | collective-permute-start | bytes 786440 | tf_op jit(solution)/shard_map/ppermute | solution.py:590
  8.1 0.0 copy-done
  8.1 0.0 copy-done.6
  8.1 0.0 copy-done.7
  8.1 0.0 copy-start.2
  8.1 0.0 copy-start.3
  8.1 0.0 copy-start.4
  8.1 0.0 copy-start.5
  8.1 2.9 %inner.1 = (bf16[2,2,768,256]{3,2,1,0:T(8,128)(2,1)S(1)}, f32[40,128]{1,0:T(8,128)S(1)}) custom-call(f32[8,320,128]{2,1,0:T(8,128)S(1)} %bitcast.4, s32[2,8,16]{2,1,0:T(8,128)S(1)} %copy-done.6, s32[8,128]{1,0:T(8,128)S(1)} %copy-done.7, bf16[2,8,16,128,128]{4,3,2,1,0:T(8,128)(2,1)} %tiles_ref.3), custom_call_target="tpu_custom_call" | custom-call | flops 33554432 | bytes 4194304 | tf_op jit(solution)/shard_map/inner/pallas_call | solution.py:592
  11.1 1.4 %collective-permute-done.from_left = bf16[2,512,128]{2,1,0:T(8,128)(2,1)S(1)} collective-permute-done((bf16[2,512,128]{2,1,0:T(8,128)(2,1)}, bf16[2,512,128]{2,1,0:T(8,128)(2,1)S(1)}, u32[]{:S(2)}, u32[]{:S(2)}) %collective-permute-start) | collective-permute-done | bytes 262176 | tf_op jit(solution)/shard_map/ppermute | solution.py:591
  12.4 2.6 %collective-permute-done.1.from_right = bf16[2,512,128]{2,1,0:T(8,128)(2,1)S(1)} collective-permute-done((bf16[2,512,128]{2,1,0:T(8,128)(2,1)}, bf16[2,512,128]{2,1,0:T(8,128)(2,1)S(1)}, u32[]{:S(2)}, u32[]{:S(2)}) %collective-permute-start.1) | collective-permute-done | bytes 262176 | tf_op jit(solution)/shard_map/ppermute | solution.py:590
  15.0 0.0 copy-done.1
  15.0 0.0 copy-done.2
  15.0 0.0 copy-done.3
  15.0 0.0 copy-done.4
  15.0 0.0 copy-done.5
  15.1 39.6 %steps.1 = (f32[320,128]{1,0:T(8,128)S(1)}, f32[9]{0:T(128)S(1)}) custom-call(f32[2,32,1024]{2,1,0:T(8,128)S(1)} %copy-done.3, bf16[2,32,1024]{2,1,0:T(8,128)(2,1)S(1)} %copy-done.4, f32[320,128]{1,0:T(8,128)S(1)} %bitcast.7, f32[20,20]{1,0:T(8,128)S(1)} %copy-done.5, bf16[2,2,768,256]{3,2,1,0:T(8,128)(2,1)S(1)} %copy-done.1, ...), custom_call_target="tpu_custom_call" | custom-call | tf_op jit(solution)/shard_map/steps/pallas_call | solution.py:606
  54.6 0.7 %copy.11 = f32[2,20,8,128]{3,2,1,0:T(8,128)} copy(f32[2,20,8,128]{3,2,1,0:T(8,128)S(1)} %bitcast.8) | data formatting | bytes 327680
  55.3 0.5 copy.12
  (1 shorter events, 0.0 us)
Async XLA Ops:
  0.6 7.5 %copy-start = (f32[8,2,20,8,128]{4,3,2,1,0:T(8,128)S(1)}, f32[8,2,20,8,128]{4,3,2,1,0:T(8,128)}, u32[]{:S(2)}) copy-start(f32[8,2,20,8,128]{4,3,2,1,0:T(8,128)} %param.13) | copy-start | bytes 3932164
  0.6 7.5 %copy-start.6 = (s32[2,8,16]{2,1,0:T(8,128)S(1)}, s32[2,8,16]{2,1,0:T(8,128)}, u32[]{:S(2)}) copy-start(s32[2,8,16]{2,1,0:T(8,128)} %cols_ref.3) | copy-start | bytes 3076
  0.7 7.4 %copy-start.7 = (s32[8,128]{1,0:T(8,128)S(1)}, s32[8,128]{1,0:T(8,128)}, u32[]{:S(2)}) copy-start(s32[8,128]{1,0:T(8,128)} %wet_ref.3) | copy-start | bytes 12292
  5.6 6.9 %collective-permute-start = (bf16[2,512,128]{2,1,0:T(8,128)(2,1)}, bf16[2,512,128]{2,1,0:T(8,128)(2,1)S(1)}, u32[]{:S(2)}, u32[]{:S(2)}) collective-permute-start(bf16[2,512,128]{2,1,0:T(8,128)(2,1)} %get-tuple-element.15), channel_id=1, source_target_pairs={{0,1},{1,2},{2,3},{3,0},{4,5},{5,6},{6,7},{7,4},{8,9},{9,10},{10,1... | collective-permute-start | bytes 786440 | tf_op jit(solution)/shard_map/ppermute | solution.py:591
  6.1 9.0 %collective-permute-start.1 = (bf16[2,512,128]{2,1,0:T(8,128)(2,1)}, bf16[2,512,128]{2,1,0:T(8,128)(2,1)S(1)}, u32[]{:S(2)}, u32[]{:S(2)}) collective-permute-start(bf16[2,512,128]{2,1,0:T(8,128)(2,1)} %get-tuple-element.16), channel_id=1, source_target_pairs={{0,3},{1,0},{2,1},{3,2},{4,7},{5,4},{6,5},{7,6},{8,11},{9,8},{10,9... | collective-permute-start | bytes 786440 | tf_op jit(solution)/shard_map/ppermute | solution.py:590
  8.1 6.9 %copy-start.1 = (bf16[2,2,768,256]{3,2,1,0:T(8,128)(2,1)S(1)}, bf16[2,2,768,256]{3,2,1,0:T(8,128)(2,1)}, u32[]{:S(2)}) copy-start(bf16[2,2,768,256]{3,2,1,0:T(8,128)(2,1)} %get-tuple-element.13.w_edge) | copy-start | bytes 4718596
  8.1 6.9 %copy-start.2 = (f32[2,20,8,128]{3,2,1,0:T(8,128)S(1)}, f32[2,20,8,128]{3,2,1,0:T(8,128)}, u32[]{:S(2)}) copy-start(f32[2,20,8,128]{3,2,1,0:T(8,128)} %param.8) | copy-start | bytes 491524
  8.1 6.9 %copy-start.3 = (f32[2,32,1024]{2,1,0:T(8,128)S(1)}, f32[2,32,1024]{2,1,0:T(8,128)}, u32[]{:S(2)}) copy-start(f32[2,32,1024]{2,1,0:T(8,128)} %get-tuple-element.11.slope) | copy-start | bytes 786436
  8.1 6.9 %copy-start.4 = (bf16[2,32,1024]{2,1,0:T(8,128)(2,1)S(1)}, bf16[2,32,1024]{2,1,0:T(8,128)(2,1)}, u32[]{:S(2)}) copy-start(bf16[2,32,1024]{2,1,0:T(8,128)(2,1)} %get-tuple-element.12.start) | copy-start | bytes 393220
  8.1 6.9 %copy-start.5 = (f32[20,20]{1,0:T(8,128)S(1)}, f32[20,20]{1,0:T(8,128)}, u32[]{:S(2)}) copy-start(f32[20,20]{1,0:T(8,128)} %coup_ref.1) | copy-start | bytes 4804
